TPU v7x, 512 devices: a whole 4x4x16 slice. The times are simulated.
512 devices in a mesh: ctx: 64 (over y, z), smp: 8 (over x, core).
Axes of the slice: x: 4, y: 4, z: 16, core: 2. Of those that a mesh axis runs over, the one named last changes fastest.
Arguments:
- queries: bfloat16 [8, 16384, 2048], P('smp', 'ctx'), may hold values from -200 to 200
- out_grad: bfloat16 [8, 16384, 2048], P('smp', 'ctx'), may hold values from -6 to 6
- local_keys: bfloat16 [8, 16384, 512], P('smp', 'ctx'), may hold values from -4 to 4
- trajectory_values: bfloat16 [8, 16384, 512], P('smp', 'ctx'), may hold values from -6 to 6
- journal_keys: bfloat16 [64, 256, 512], P('ctx'), may hold values from -6 to 6
- journal_values: bfloat16 [64, 256, 512], P('ctx'), may hold values from -6 to 6
- picks: int32 [8, 64, 3], P('smp', 'ctx'), may hold values from 0 to 63, all different within a row
- lengths: int32 [8], P('smp'), may hold values from 1 to 16384, as said below
Outputs:
- grad_queries: bfloat16 [8, 16384, 2048], P('smp', 'ctx')
- grad_local_keys: bfloat16 [8, 16384, 512], P('smp', 'ctx')
- grad_local_values: bfloat16 [8, 16384, 512], P('smp', 'ctx')
- grad_log_keys: bfloat16 [64, 256, 512], P('ctx', None, 'smp')
- grad_log_values: bfloat16 [64, 256, 512], P('ctx', None, 'smp')
Inputs may be any that keep to these rules, and one draw needn't show every extreme that they name: `lengths`: each trajectory's length in tokens; some trajectory has all 16384 tokens. The 3 picks of a query block are different blocks.
All inputs are finite; a program needn't handle non-finite values.
Results may differ from a plain program's by a relative error of at most 0.028.
Values may be sent and summed in bfloat16 or wider, within the bound.
A program may use at most 64 MiB of HBM per device.

v0:
```python
import math

import jax
import jax.numpy as jnp
from jax import lax
from jax.sharding import PartitionSpec as P

HEAD_SIZE = 128


def head_grads(query_head, grad_head, key_head, value_head, visible):
    score_scale = 1.0 / math.sqrt(HEAD_SIZE)
    scores = (
        jnp.einsum("tgd,kd->gtk", query_head, key_head, preferred_element_type=jnp.float32)
        * score_scale
    )
    scores = jnp.where(visible[None], scores, -1e30)
    top_score = jnp.max(scores, axis=-1, keepdims=True)
    weights = jnp.exp(scores - top_score)
    probs_full = weights / jnp.sum(weights, axis=-1, keepdims=True)
    probs_low = probs_full.astype(jnp.bfloat16)
    output = jnp.einsum("gtk,kd->tgd", probs_low, value_head, preferred_element_type=jnp.float32)
    row_delta = jnp.sum(grad_head.astype(jnp.float32) * output, axis=-1)
    grad_probs = jnp.einsum(
        "tgd,kd->gtk", grad_head, value_head, preferred_element_type=jnp.float32
    )
    grad_scores = probs_full * (grad_probs - row_delta.T[:, :, None])
    grad_low = grad_scores.astype(jnp.bfloat16)
    grad_query = (
        jnp.einsum("gtk,kd->tgd", grad_low, key_head, preferred_element_type=jnp.float32)
        * score_scale
    )
    key_gradient = (
        jnp.einsum("gtk,tgd->kd", grad_low, query_head, preferred_element_type=jnp.float32)
        * score_scale
    )
    value_gradient = jnp.einsum(
        "gtk,tgd->kd", probs_low, grad_head, preferred_element_type=jnp.float32
    )
    return (grad_query, key_gradient, value_gradient)


def block_grads(
    block_of_queries, block_gradient, block_of_keys, block_of_values, visible, kv_heads
):
    tq_rows = block_of_queries.shape[0]
    count_of_keys = block_of_keys.shape[0]
    head_group = block_of_queries.shape[1] // (kv_heads * HEAD_SIZE)
    heads_of_queries = block_of_queries.reshape(tq_rows, kv_heads, head_group, HEAD_SIZE).transpose(
        1, 0, 2, 3
    )
    heads_gradient = block_gradient.reshape(tq_rows, kv_heads, head_group, HEAD_SIZE).transpose(
        1, 0, 2, 3
    )
    heads_of_keys = block_of_keys.reshape(count_of_keys, kv_heads, HEAD_SIZE).transpose(1, 0, 2)
    heads_of_values = block_of_values.reshape(count_of_keys, kv_heads, HEAD_SIZE).transpose(1, 0, 2)
    grad_query, key_gradient, value_gradient = lax.map(
        lambda head_parts: head_grads(
            head_parts[0], head_parts[1], head_parts[2], head_parts[3], visible
        ),
        (heads_of_queries, heads_gradient, heads_of_keys, heads_of_values),
    )
    grad_query = grad_query.transpose(1, 0, 2, 3).reshape(
        tq_rows, kv_heads * head_group * HEAD_SIZE
    )
    key_gradient = key_gradient.transpose(1, 0, 2).reshape(count_of_keys, kv_heads * HEAD_SIZE)
    value_gradient = value_gradient.transpose(1, 0, 2).reshape(count_of_keys, kv_heads * HEAD_SIZE)
    return (grad_query.astype(jnp.bfloat16), key_gradient, value_gradient)


def body(
    queries, out_grad, local_keys, trajectory_values, journal_keys, journal_values, picks, lengths
):
    ctx_size = lax.axis_size("ctx")
    ctx_index = lax.axis_index("ctx")
    tq_rows = queries.shape[1]
    feature_axis = local_keys.shape[2]
    kv_heads = feature_axis // HEAD_SIZE
    top_count = picks.shape[2]
    block_rows = journal_keys.shape[1]
    piece_rows = block_rows // ctx_size
    split_row = top_count * block_rows
    strips = (
        lax.all_to_all(
            journal_keys.reshape(1, ctx_size, piece_rows, feature_axis),
            "ctx",
            split_axis=1,
            concat_axis=0,
            tiled=True,
        ),
        lax.all_to_all(
            journal_values.reshape(1, ctx_size, piece_rows, feature_axis),
            "ctx",
            split_axis=1,
            concat_axis=0,
            tiled=True,
        ),
    )
    strip_keys = strips[0].reshape(ctx_size, piece_rows, feature_axis)
    strip_values = strips[1].reshape(ctx_size, piece_rows, feature_axis)
    wanted = lax.all_gather(picks[0], "ctx", axis=0, tiled=True)
    pick_order = wanted.T
    fetched = (
        lax.all_to_all(strip_keys[pick_order], "ctx", split_axis=1, concat_axis=1, tiled=True),
        lax.all_to_all(strip_values[pick_order], "ctx", split_axis=1, concat_axis=1, tiled=True),
    )
    block_of_keys = jnp.concatenate(
        [fetched[0].reshape(split_row, feature_axis), local_keys[0]], axis=0
    )
    block_of_values = jnp.concatenate(
        [fetched[1].reshape(split_row, feature_axis), trajectory_values[0]], axis=0
    )
    first_row = ctx_index * tq_rows
    live_rows = first_row + jnp.arange(tq_rows, dtype=jnp.int32) < lengths[0]
    block_gradient = jnp.where(live_rows[:, None], out_grad[0], jnp.zeros_like(out_grad[0]))
    causal = (
        jnp.arange(tq_rows, dtype=jnp.int32)[:, None]
        >= jnp.arange(tq_rows, dtype=jnp.int32)[None, :]
    )
    visible = jnp.concatenate([jnp.ones((tq_rows, split_row), dtype=bool), causal], axis=1)
    grad_query, key_gradient, value_gradient = block_grads(
        queries[0], block_gradient, block_of_keys, block_of_values, visible, kv_heads
    )
    log_key_grad = key_gradient[:split_row].reshape(top_count, ctx_size, piece_rows, feature_axis)
    log_value_grad = value_gradient[:split_row].reshape(
        top_count, ctx_size, piece_rows, feature_axis
    )
    returned = (
        lax.all_to_all(log_key_grad, "ctx", split_axis=1, concat_axis=1, tiled=True),
        lax.all_to_all(log_value_grad, "ctx", split_axis=1, concat_axis=1, tiled=True),
    )
    selector = (
        pick_order.reshape(-1)[None, :] == jnp.arange(ctx_size, dtype=jnp.int32)[:, None]
    ).astype(jnp.float32)
    dense_keys = jnp.dot(
        selector,
        returned[0].reshape(top_count * ctx_size, piece_rows * feature_axis),
        precision=lax.Precision.HIGHEST,
        preferred_element_type=jnp.float32,
    )
    dense_values = jnp.dot(
        selector,
        returned[1].reshape(top_count * ctx_size, piece_rows * feature_axis),
        precision=lax.Precision.HIGHEST,
        preferred_element_type=jnp.float32,
    )
    dense_keys = dense_keys.reshape(ctx_size, piece_rows, feature_axis)
    dense_values = dense_values.reshape(ctx_size, piece_rows, feature_axis)
    owned = (
        lax.all_to_all(dense_keys, "ctx", split_axis=0, concat_axis=1, tiled=True),
        lax.all_to_all(dense_values, "ctx", split_axis=0, concat_axis=1, tiled=True),
    )
    summed = (
        lax.psum_scatter(owned[0], "smp", scatter_dimension=2, tiled=True),
        lax.psum_scatter(owned[1], "smp", scatter_dimension=2, tiled=True),
    )
    return (
        grad_query[None],
        key_gradient[split_row:].astype(jnp.bfloat16)[None],
        value_gradient[split_row:].astype(jnp.bfloat16)[None],
        summed[0].astype(jnp.bfloat16),
        summed[1].astype(jnp.bfloat16),
    )


def solution(mesh):
    in_specs = (
        P("smp", "ctx", None),
        P("smp", "ctx", None),
        P("smp", "ctx", None),
        P("smp", "ctx", None),
        P("ctx", None, None),
        P("ctx", None, None),
        P("smp", "ctx", None),
        P("smp"),
    )
    out_specs = (
        P("smp", "ctx", None),
        P("smp", "ctx", None),
        P("smp", "ctx", None),
        P("ctx", None, "smp"),
        P("ctx", None, "smp"),
    )
    return jax.shard_map(body, mesh=mesh, in_specs=in_specs, out_specs=out_specs, check_vma=False)
```

profile of v0, /device:TPU:7, one launch (start us, length us, event | category | flops | bytes accessed | tf_op | source)
XLA Modules:
  0.0 574.4 jit_solution(7148500020277334877)
XLA Ops:
  0.6 1.7 reshape.125
  2.4 18.5 %all-to-all-start.2 = ((bf16[1,64,4,512]{3,2,0,1:T(4,128)(2,1)}), bf16[1,64,4,512]{3,2,0,1:T(4,128)(2,1)S(1)}, u32[]{:S(2)}, u32[]{:S(2)}) async-start(bf16[1,64,4,512]{3,2,0,1:T(4,128)(2,1)} %reshape.125), calls=%async_computation.2 | async-start | bytes 524288 | tf_op jit(solution)/shard_map/all_to_all | solution.py:91
  20.8 1.7 reshape.123
  22.5 17.3 %all-to-all-done.2 = bf16[1,64,4,512]{3,2,0,1:T(4,128)(2,1)S(1)} async-done(((bf16[1,64,4,512]{3,2,0,1:T(4,128)(2,1)}), bf16[1,64,4,512]{3,2,0,1:T(4,128)(2,1)S(1)}, u32[]{:S(2)}, u32[]{:S(2)}) %all-to-all-start.2) | async-done | bytes 262176 | tf_op jit(solution)/shard_map/all_to_all | solution.py:91
  39.9 7.6 %all-to-all-start = ((bf16[1,64,4,512]{3,2,0,1:T(4,128)(2,1)}), bf16[1,64,4,512]{3,2,0,1:T(4,128)(2,1)S(1)}, u32[]{:S(2)}, u32[]{:S(2)}) async-start(bf16[1,64,4,512]{3,2,0,1:T(4,128)(2,1)} %reshape.123), calls=%async_computation | async-start | bytes 524288 | tf_op jit(solution)/shard_map/all_to_all | solution.py:84
  47.5 65.6 %all-gather = s32[64,1,3]{2,1,0:T(1,128)S(1)} all-gather(s32[1,1,3]{2,1,0:T(1,128)S(1)} %copy-done.8), channel_id=2, replica_groups=mesh['ctx'=64,'smp'=8] {'ctx'}, dimensions={0}, use_global_device_ids=true | all-gather | bytes 780 | tf_op jit(solution)/shard_map/all_gather | solution.py:101
  115.7 8.6 %all-to-all-start.3 = ((bf16[3,64,4,512]{3,2,0,1:T(4,128)(2,1)}), bf16[3,64,4,512]{3,2,0,1:T(4,128)(2,1)S(1)}, u32[]{:S(2)}, u32[]{:S(2)}) async-start(bf16[3,64,4,512]{3,2,0,1:T(4,128)(2,1)} %copy.96), calls=%async_computation.3 | async-start | bytes 1572864 | tf_op jit(solution)/shard_map/all_to_all | solution.py:105
  126.8 22.5 %all-to-all-done.3 = bf16[3,64,4,512]{3,2,0,1:T(4,128)(2,1)S(1)} async-done(((bf16[3,64,4,512]{3,2,0,1:T(4,128)(2,1)}), bf16[3,64,4,512]{3,2,0,1:T(4,128)(2,1)S(1)}, u32[]{:S(2)}, u32[]{:S(2)}) %all-to-all-start.3) | async-done | bytes 786464 | tf_op jit(solution)/shard_map/all_to_all | solution.py:105
  149.4 8.2 %all-to-all-start.1 = ((bf16[3,64,4,512]{3,2,0,1:T(4,128)(2,1)}), bf16[3,64,4,512]{3,2,0,1:T(4,128)(2,1)}, u32[]{:S(2)}, u32[]{:S(2)}) async-start(bf16[3,64,4,512]{3,2,0,1:T(4,128)(2,1)} %copy.91), calls=%async_computation.1 | async-start | bytes 1572864 | tf_op jit(solution)/shard_map/all_to_all | solution.py:104
  160.2 1.5 copy.100
  164.0 22.1 %all-to-all-done.1 = bf16[3,64,4,512]{3,2,0,1:T(4,128)(2,1)} async-done(((bf16[3,64,4,512]{3,2,0,1:T(4,128)(2,1)}), bf16[3,64,4,512]{3,2,0,1:T(4,128)(2,1)}, u32[]{:S(2)}, u32[]{:S(2)}) %all-to-all-start.1) | async-done | bytes 786464 | tf_op jit(solution)/shard_map/all_to_all | solution.py:104
  188.7 1.9 maximum_bitcast_fusion
  191.7 60.7 %while.14 = (s32[]{:T(128)}, bf16[4,256,4,128]{1,3,2,0:T(8,128)(2,1)}, f32[4,1024,128]{2,1,0:T(8,128)}, f32[4,1024,128]{2,1,0:T(8,128)}, bf16[4,1024,128]{2,1,0:...) while((s32[]{:T(128)}, ...), condition=%wide.region_4.5_spmd, body=%wide.region_0.4_spmd.sunk | while | flops 1621753856 | bytes 55600328 | solution.py:57
  191.9 4.5 fusion.112
  196.4 2.5 fusion.113
  200.0 1.5 fusion.118
  202.7 1.4 fusion.116
  204.2 2.7 fusion.117
  207.0 4.5 fusion.112
  211.5 2.5 fusion.113
  215.1 1.5 fusion.118
  217.8 1.4 fusion.116
  219.3 2.7 fusion.117
  222.2 4.5 fusion.112
  226.7 2.5 fusion.113
  230.3 1.5 fusion.118
  233.0 1.4 fusion.116
  234.4 2.7 fusion.117
  237.3 4.5 fusion.112
  241.8 2.5 fusion.113
  245.4 1.6 fusion.118
  248.2 1.4 fusion.116
  249.7 2.7 fusion.117
  252.3 1.5 slice.29
  255.8 1.4 copy.116
  257.2 6.9 %all-to-all-start.6 = ((f32[3,64,4,512]{3,2,0,1:T(4,128)}), f32[3,64,4,512]{3,2,0,1:T(4,128)S(1)}, u32[]{:S(2)}, u32[]{:S(2)}) async-start(f32[3,64,4,512]{3,2,0,1:T(4,128)} %copy.116), calls=%async_computation.6 | async-start | bytes 3145728 | tf_op jit(solution)/shard_map/all_to_all | solution.py:130
  264.1 1.5 slice.28
  266.6 2.1 reshape.127
  268.8 2.8 copy.110
  271.6 42.7 %all-to-all-done.6 = f32[3,64,4,512]{3,2,0,1:T(4,128)S(1)} async-done(((f32[3,64,4,512]{3,2,0,1:T(4,128)}), f32[3,64,4,512]{3,2,0,1:T(4,128)S(1)}, u32[]{:S(2)}, u32[]{:S(2)}) %all-to-all-start.6) | async-done | bytes 1572896 | tf_op jit(solution)/shard_map/all_to_all | solution.py:130
  314.3 11.9 %all-to-all-start.4 = ((f32[3,64,4,512]{3,2,0,1:T(4,128)}), f32[3,64,4,512]{3,2,0,1:T(4,128)S(1)}, u32[]{:S(2)}, u32[]{:S(2)}) async-start(f32[3,64,4,512]{3,2,0,1:T(4,128)} %copy.110), calls=%async_computation.4 | async-start | bytes 3145728 | tf_op jit(solution)/shard_map/all_to_all | solution.py:129
  329.0 53.2 %all-to-all-done.4 = f32[3,64,4,512]{3,2,0,1:T(4,128)S(1)} async-done(((f32[3,64,4,512]{3,2,0,1:T(4,128)}), f32[3,64,4,512]{3,2,0,1:T(4,128)S(1)}, u32[]{:S(2)}, u32[]{:S(2)}) %all-to-all-start.4) | async-done | bytes 1572896 | tf_op jit(solution)/shard_map/all_to_all | solution.py:129
  382.2 10.5 %all-to-all-start.7 = ((f32[64,4,512]{2,1,0:T(4,128)}), f32[64,4,512]{2,1,0:T(4,128)S(1)}, u32[]{:S(2)}, u32[]{:S(2)}) async-start(f32[64,4,512]{2,1,0:T(4,128)} %copy.119), calls=%async_computation.7 | async-start | bytes 1048576 | tf_op jit(solution)/shard_map/all_to_all | solution.py:151
  395.3 24.0 %all-to-all-done.7 = f32[64,4,512]{2,1,0:T(4,128)S(1)} async-done(((f32[64,4,512]{2,1,0:T(4,128)}), f32[64,4,512]{2,1,0:T(4,128)S(1)}, u32[]{:S(2)}, u32[]{:S(2)}) %all-to-all-start.7) | async-done | bytes 524320 | tf_op jit(solution)/shard_map/all_to_all | solution.py:151
  419.3 7.1 %all-to-all-start.5 = ((f32[64,4,512]{2,1,0:T(4,128)}), f32[64,4,512]{2,1,0:T(4,128)S(1)}, u32[]{:S(2)}, u32[]{:S(2)}) async-start(f32[64,4,512]{2,1,0:T(4,128)} %copy.113), calls=%async_computation.5 | async-start | bytes 1048576 | tf_op jit(solution)/shard_map/all_to_all | solution.py:150
  430.5 1.4 copy.130
  434.5 20.6 %all-to-all-done.5 = f32[64,4,512]{2,1,0:T(4,128)S(1)} async-done(((f32[64,4,512]{2,1,0:T(4,128)}), f32[64,4,512]{2,1,0:T(4,128)S(1)}, u32[]{:S(2)}, u32[]{:S(2)}) %all-to-all-start.5) | async-done | bytes 524320 | tf_op jit(solution)/shard_map/all_to_all | solution.py:150
  455.7 117.2 %all-reduce.5 = (bf16[1,256,512]{1,0,2:T(2,128)(2,1)S(1)}, bf16[1,256,512]{1,0,2:T(2,128)(2,1)S(1)}) all-reduce(f32[1,256,512]{1,0,2:T(1,128)S(1)} %copy.114, f32[1,256,512]{1,0,2:T(1,128)S(1)} %copy.120), channel_id=3, replica_groups=mesh['ctx'=64,'smp'=8] {'smp'}, use_global_device_ids=true, to_apply=%region_5.6.clone | all-reduce | flops 262144 | bytes 1572864
  (105 shorter events, 39.1 us)
Async XLA Ops:
  0.6 46.9 %copy-start.8 = (s32[1,1,3]{2,1,0:T(1,128)S(1)}, s32[1,1,3]{2,1,0:T(1,128)}, u32[]{:S(2)}) copy-start(s32[1,1,3]{2,1,0:T(1,128)} %param.16) | copy-start | bytes 40
  2.4 37.5 %all-to-all-start.2 = ((bf16[1,64,4,512]{3,2,0,1:T(4,128)(2,1)}), bf16[1,64,4,512]{3,2,0,1:T(4,128)(2,1)S(1)}, u32[]{:S(2)}, u32[]{:S(2)}) async-start(bf16[1,64,4,512]{3,2,0,1:T(4,128)(2,1)} %reshape.125), calls=%async_computation.2 | async-start | bytes 524288 | tf_op jit(solution)/shard_map/all_to_all | solution.py:91
  39.9 75.8 %all-to-all-start = ((bf16[1,64,4,512]{3,2,0,1:T(4,128)(2,1)}), bf16[1,64,4,512]{3,2,0,1:T(4,128)(2,1)S(1)}, u32[]{:S(2)}, u32[]{:S(2)}) async-start(bf16[1,64,4,512]{3,2,0,1:T(4,128)(2,1)} %reshape.123), calls=%async_computation | async-start | bytes 524288 | tf_op jit(solution)/shard_map/all_to_all | solution.py:84
  115.7 33.7 %all-to-all-start.3 = ((bf16[3,64,4,512]{3,2,0,1:T(4,128)(2,1)}), bf16[3,64,4,512]{3,2,0,1:T(4,128)(2,1)S(1)}, u32[]{:S(2)}, u32[]{:S(2)}) async-start(bf16[3,64,4,512]{3,2,0,1:T(4,128)(2,1)} %copy.96), calls=%async_computation.3 | async-start | bytes 1572864 | tf_op jit(solution)/shard_map/all_to_all | solution.py:105
  124.3 33.9 %copy-start.6 = (bf16[1,256,512]{2,1,0:T(8,128)(2,1)S(1)}, bf16[1,256,512]{2,1,0:T(8,128)(2,1)}, u32[]{:S(2)}) copy-start(bf16[1,256,512]{2,1,0:T(8,128)(2,1)} %param.12) | copy-start | bytes 786436
  125.6 32.9 %copy-start.7 = (bf16[1,256,512]{2,1,0:T(8,128)(2,1)S(1)}, bf16[1,256,512]{2,1,0:T(8,128)(2,1)}, u32[]{:S(2)}) copy-start(bf16[1,256,512]{2,1,0:T(8,128)(2,1)} %param.13) | copy-start | bytes 786436
  126.8 32.1 %copy-start.1 = (bf16[1,256,2048]{2,1,0:T(8,128)(2,1)S(1)}, bf16[1,256,2048]{2,1,0:T(8,128)(2,1)}, u32[]{:S(2)}) copy-start(bf16[1,256,2048]{2,1,0:T(8,128)(2,1)} %param.10) | copy-start | bytes 3145732
  149.4 36.7 %all-to-all-start.1 = ((bf16[3,64,4,512]{3,2,0,1:T(4,128)(2,1)}), bf16[3,64,4,512]{3,2,0,1:T(4,128)(2,1)}, u32[]{:S(2)}, u32[]{:S(2)}) async-start(bf16[3,64,4,512]{3,2,0,1:T(4,128)(2,1)} %copy.91), calls=%async_computation.1 | async-start | bytes 1572864 | tf_op jit(solution)/shard_map/all_to_all | solution.py:104
  188.7 3.0 copy-start.5
  198.9 2.6 copy-start
  201.5 1.2 copy-start.2
  204.1 2.7 copy-start.3
  214.0 2.6 copy-start
  216.6 1.2 copy-start.2
  219.3 2.7 copy-start.3
  229.2 2.6 copy-start
  231.8 1.2 copy-start.2
  234.4 2.7 copy-start.3
  244.4 2.6 copy-start
  247.0 1.2 copy-start.2
  249.7 2.7 copy-start.3
  257.2 57.1 %all-to-all-start.6 = ((f32[3,64,4,512]{3,2,0,1:T(4,128)}), f32[3,64,4,512]{3,2,0,1:T(4,128)S(1)}, u32[]{:S(2)}, u32[]{:S(2)}) async-start(f32[3,64,4,512]{3,2,0,1:T(4,128)} %copy.116), calls=%async_computation.6 | async-start | bytes 3145728 | tf_op jit(solution)/shard_map/all_to_all | solution.py:130
  314.3 67.8 %all-to-all-start.4 = ((f32[3,64,4,512]{3,2,0,1:T(4,128)}), f32[3,64,4,512]{3,2,0,1:T(4,128)S(1)}, u32[]{:S(2)}, u32[]{:S(2)}) async-start(f32[3,64,4,512]{3,2,0,1:T(4,128)} %copy.110), calls=%async_computation.4 | async-start | bytes 3145728 | tf_op jit(solution)/shard_map/all_to_all | solution.py:129
  382.2 37.1 %all-to-all-start.7 = ((f32[64,4,512]{2,1,0:T(4,128)}), f32[64,4,512]{2,1,0:T(4,128)S(1)}, u32[]{:S(2)}, u32[]{:S(2)}) async-start(f32[64,4,512]{2,1,0:T(4,128)} %copy.119), calls=%async_computation.7 | async-start | bytes 1048576 | tf_op jit(solution)/shard_map/all_to_all | solution.py:151
  394.1 36.3 %copy-start.4 = (bf16[4,256,4,128]{1,3,2,0:T(8,128)(2,1)S(1)}, bf16[4,256,4,128]{1,3,2,0:T(8,128)(2,1)}, u32[]{:S(2)}) copy-start(bf16[4,256,4,128]{1,3,2,0:T(8,128)(2,1)} %get-tuple-element.54) | copy-start | bytes 3145732
  419.3 35.9 %all-to-all-start.5 = ((f32[64,4,512]{2,1,0:T(4,128)}), f32[64,4,512]{2,1,0:T(4,128)S(1)}, u32[]{:S(2)}, u32[]{:S(2)}) async-start(f32[64,4,512]{2,1,0:T(4,128)} %copy.113), calls=%async_computation.5 | async-start | bytes 1048576 | tf_op jit(solution)/shard_map/all_to_all | solution.py:150
where the time goes:
time: 577 us; the launch traced here: 574 us
  waiting for transfers between devices  202 us (35%)
  blocking collectives  183 us (32%)
  starting transfers between devices  79.3 us (14%)
  matrix products  49.8 us (9%)
  local copies, waits for them, and re-layouts  44.7 us (8%)
  other arithmetic  12.8 us (2%)
    unnamed x1, blocking collectives  117 us
    all_gather x1, blocking collectives, body(): wanted = lax.all_gather(picks[0], 'ctx', axis=0, tiled=True)  65.6 us
    all_to_all x1, waiting for transfers between devices, body(): lax.all_to_all(log_key_grad, 'ctx', split_axis=1, concat_axis=1, tiled=True)  53.2 us
    all_to_all x1, waiting for transfers between devices, body(): lax.all_to_all(log_value_grad, 'ctx', split_axis=1, concat_axis=1, tiled=...  42.7 us
    all_to_all x1, waiting for transfers between devices, body(): lax.all_to_all(dense_values, 'ctx', split_axis=0, concat_axis=1, tiled=True)  24 us
    all_to_all x1, waiting for transfers between devices, body(): lax.all_to_all(strip_values[pick_order], 'ctx', split_axis=1, concat_axis...  22.5 us
    all_to_all x1, waiting for transfers between devices, body(): lax.all_to_all(strip_keys[pick_order], 'ctx', split_axis=1, concat_axis=1...  22.1 us
    all_to_all x1, waiting for transfers between devices, body(): lax.all_to_all(dense_keys, 'ctx', split_axis=0, concat_axis=1, tiled=True)  20.6 us
  transfers between devices with their start and end apart: 8, of which 7 were waited for; matrix products, arithmetic and copies ran while one was open for 6% of the time, Pallas kernels for 0%

commit v1 on v0

v1 whole, which is shorter than its diff:
```python
import functools
import math

import jax
import jax.numpy as jnp
from jax import lax
from jax.experimental import pallas as pl
from jax.experimental.pallas import tpu as pltpu
from jax.sharding import PartitionSpec as P

HEAD = 128
Y_CHIPS = 4
SCALE = 1.0 / math.sqrt(HEAD)
MESH = pl.DeviceIdType.MESH
BF16 = jnp.bfloat16
F32 = jnp.float32


def place(z_chips):
    ctx = lax.axis_index("ctx")
    return ctx // z_chips, ctx % z_chips, lax.axis_index("smp")


def peer_of(offset, y, smp, smp_size):
    half = smp_size // 2
    ds = offset % smp_size
    py = (y + offset // smp_size) % Y_CHIPS
    px = (smp // 2 + ds // 2) % half
    pc = (smp + ds) % 2
    return py, px * 2 + pc


def source_of(offset, y, smp, smp_size):
    half = smp_size // 2
    ds = offset % smp_size
    py = (y + Y_CHIPS - offset // smp_size) % Y_CHIPS
    px = (smp // 2 + half - ds // 2) % half
    pc = (smp + ds) % 2
    return py, px * 2 + pc


def enter(y, z, smp, z_chips, smp_size):
    barrier = pltpu.get_barrier_semaphore()
    count = Y_CHIPS * smp_size

    def greet(offset, carry):
        py, ps = peer_of(offset, y, smp, smp_size)
        pl.semaphore_signal(barrier, 1, device_id=(py * z_chips + z, ps), device_id_type=MESH)
        return carry

    for step in (1, z_chips - 1):
        pl.semaphore_signal(
            barrier,
            1,
            device_id=(y * z_chips + (z + step) % z_chips, smp),
            device_id_type=MESH,
        )
    lax.fori_loop(1, count, greet, 0)
    pl.semaphore_wait(barrier, count + 1)


def fetch_kernel(
    z_chips,
    smp_size,
    picks_ref,
    keys_ref,
    values_ref,
    out_ref,
    where_ref,
    log,
    staged,
    named,
    named_s,
    spread_send,
    spread_recv,
    own_sem,
    name_send,
    name_recv,
    smem_sem,
    ring_send,
    ring_recv,
    pick_send,
    pick_recv,
):
    y, z, smp = place(z_chips)
    planes = Y_CHIPS * smp_size
    mine = y * smp_size + smp
    rows = log.shape[2]
    cols = log.shape[3]
    per_array = planes // 2
    lane = lax.broadcasted_iota(jnp.int32, (1, 128), 1)
    named[mine] = jnp.where(
        lane == 0,
        picks_ref[0, 0, 0],
        jnp.where(lane == 1, picks_ref[0, 0, 1], picks_ref[0, 0, 2]),
    )
    enter(y, z, smp, z_chips, smp_size)

    def piece(ref, owner, c):
        row = pl.multiple_of((owner % per_array) * rows, rows)
        return ref.at[0, pl.ds(row, rows), pl.ds(c * cols, cols)]

    def spread(py, c, ref):
        return pltpu.make_async_remote_copy(
            src_ref=piece(ref, py * smp_size + smp, c),
            dst_ref=log.at[c, z * Y_CHIPS + y],
            send_sem=spread_send.at[c, py],
            recv_sem=spread_recv.at[c, y],
            device_id=(py * z_chips + z, smp),
            device_id_type=MESH,
        )

    def arrived(py, c):
        return pltpu.make_async_remote_copy(
            src_ref=piece(keys_ref, mine, c),
            dst_ref=log.at[c, z * Y_CHIPS + py],
            send_sem=spread_send.at[c, py],
            recv_sem=spread_recv.at[c, py],
            device_id=(py * z_chips + z, smp),
            device_id_type=MESH,
        )

    def own(c, ref):
        return pltpu.make_async_copy(
            piece(ref, mine, c), log.at[c, z * Y_CHIPS + y], own_sem.at[c]
        )

    for c in range(2):
        for dy in range(1, Y_CHIPS):
            py = (y + dy) % Y_CHIPS

            @pl.when(py < Y_CHIPS // 2)
            def _():
                spread(py, c, keys_ref).start()

            @pl.when(py >= Y_CHIPS // 2)
            def _():
                spread(py, c, values_ref).start()

        @pl.when(y < Y_CHIPS // 2)
        def _():
            own(c, keys_ref).start()

        @pl.when(y >= Y_CHIPS // 2)
        def _():
            own(c, values_ref).start()

    def name(target, slot_send, slot_recv):
        py, ps = target
        return pltpu.make_async_remote_copy(
            src_ref=named.at[mine],
            dst_ref=named.at[slot_recv],
            send_sem=name_send.at[slot_send],
            recv_sem=name_recv.at[slot_recv],
            device_id=(py * z_chips + z, ps),
            device_id_type=MESH,
        )

    def tell(offset, carry):
        py, ps = peer_of(offset, y, smp, smp_size)
        name((py, ps), py * smp_size + ps, mine).start()
        return carry

    lax.fori_loop(1, planes, tell, 0)

    def ring(c, way, step):
        slot = (z + z_chips - step) % z_chips if way == 0 else (z + step) % z_chips
        to = (z + 1) % z_chips if way == 0 else (z + z_chips - 1) % z_chips
        part = log.at[c, pl.ds(slot * Y_CHIPS, Y_CHIPS)]
        return pltpu.make_async_remote_copy(
            src_ref=part,
            dst_ref=part,
            send_sem=ring_send.at[c, way, min(step, z_chips // 2 - 1)],
            recv_sem=ring_recv.at[c, slot],
            device_id=(y * z_chips + to, smp),
            device_id_type=MESH,
        )

    for c in range(2):
        for dy in range(1, Y_CHIPS):
            arrived((y + dy) % Y_CHIPS, c).wait_recv()
        own(c, keys_ref).wait()
        for way in range(2):
            ring(c, way, 0).start()
    half = z_chips // 2
    for step in range(1, half + 1):
        for c in range(2):
            for way in range(2):
                last = half if way == c else half - 1
                if step <= last:
                    arriving = ring(c, way, step)
                    arriving.wait_recv()
                    if step < last:
                        arriving.start()

    def told(offset, carry):
        py, ps = source_of(offset, y, smp, smp_size)
        name((py, ps), py * smp_size + ps, py * smp_size + ps).wait_recv()
        return carry

    lax.fori_loop(1, planes, told, 0)
    to_smem = pltpu.make_async_copy(named, named_s, smem_sem)
    to_smem.start()
    to_smem.wait()

    def give(c, target, slot_send, slot_recv):
        py, ps = target
        return pltpu.make_async_remote_copy(
            src_ref=staged.at[c, slot_send],
            dst_ref=out_ref.at[c, slot_recv],
            send_sem=pick_send.at[c, slot_send],
            recv_sem=pick_recv.at[c, slot_recv],
            device_id=(py * z_chips + z, ps),
            device_id_type=MESH,
        )

    def stage(target):
        for i in range(3):
            block = named_s[target, 0, i]
            at = (block % z_chips) * Y_CHIPS + block // z_chips
            for c in range(2):
                staged[c, target, i] = log[c, at]

    def send_picks(offset, carry):
        py, ps = peer_of(offset, y, smp, smp_size)
        target = py * smp_size + ps
        stage(target)
        for c in range(2):
            give(c, (py, ps), target, mine).start()
        return carry

    lax.fori_loop(1, planes, send_picks, 0)
    stage(mine)
    keep = [
        pltpu.make_async_copy(staged.at[c, mine], out_ref.at[c, mine], own_sem.at[c])
        for c in range(2)
    ]
    for c in range(2):
        keep[c].start()

    def locate(k, carry):
        found = jnp.full((1, 128), 3 * planes, jnp.int32)
        for i in range(3):
            found = jnp.where(lane == named_s[k, 0, i], 3 * k + i, found)
        where_ref[k] = found
        return carry

    lax.fori_loop(0, planes, locate, 0)

    for c in range(2):
        for dy in range(1, Y_CHIPS):
            spread((y + dy) % Y_CHIPS, c, keys_ref).wait_send()
        for way in range(2):
            for step in range(half if way == c else half - 1):
                ring(c, way, step).wait_send()

    def finish(offset, carry):
        py, ps = peer_of(offset, y, smp, smp_size)
        target = py * smp_size + ps
        name((py, ps), target, mine).wait_send()
        for c in range(2):
            give(c, (py, ps), target, mine).wait_send()
        sy, ss = source_of(offset, y, smp, smp_size)
        source = sy * smp_size + ss
        for c in range(2):
            give(c, (sy, ss), source, source).wait_recv()
        return carry

    lax.fori_loop(1, planes, finish, 0)
    for c in range(2):
        keep[c].wait()


def grads_kernel(
    length_ref,
    queries_ref,
    grad_ref,
    own_keys_ref,
    own_values_ref,
    fetched_ref,
    grad_queries_ref,
    grad_keys_ref,
    grad_values_ref,
    strips_ref,
    scores,
    grad_probs,
):
    tq = queries_ref.shape[1]
    group = queries_ref.shape[2] // HEAD
    width = group * tq
    planes = fetched_ref.shape[1]
    half = planes // 2
    live_rows = length_ref[0] - lax.axis_index("ctx") * tq
    live = lax.broadcasted_iota(jnp.int32, (tq, HEAD), 0) < live_rows
    heads_q = []
    heads_g = []
    for h in range(group):
        heads_q.append(queries_ref[0, :, h * HEAD : (h + 1) * HEAD])
        raw = grad_ref[0, :, h * HEAD : (h + 1) * HEAD]
        heads_g.append(jnp.where(live, raw, jnp.zeros_like(raw)))
    q = jnp.concatenate(heads_q, axis=0)
    g = jnp.concatenate(heads_g, axis=0)

    def keys_of(i):
        if i == 3:
            return own_keys_ref[0]
        return fetched_ref[0, :half, i].reshape(tq, HEAD)

    def values_of(i):
        if i == 3:
            return own_values_ref[0]
        return fetched_ref[0, half:, i].reshape(tq, HEAD)

    across = (((1,), (1,)), ((), ()))
    top = None
    for i in range(4):
        s = lax.dot_general(keys_of(i), q, across, preferred_element_type=F32)
        if i == 3:
            row = lax.broadcasted_iota(jnp.int32, (tq, width), 0)
            col = lax.broadcasted_iota(jnp.int32, (tq, width), 1) % tq
            s = jnp.where(col >= row, s, -1e30)
        scores[i] = s
        best = jnp.max(s, axis=0, keepdims=True)
        top = best if top is None else jnp.maximum(top, best)
        grad_probs[i] = lax.dot_general(values_of(i), g, across, preferred_element_type=F32)
    total = jnp.zeros((1, width), F32)
    delta = jnp.zeros((1, width), F32)
    for i in range(4):
        w = jnp.exp((scores[i] - top) * SCALE)
        scores[i] = w
        total = total + jnp.sum(w, axis=0, keepdims=True)
        delta = delta + jnp.sum(w * grad_probs[i], axis=0, keepdims=True)
    inverse = 1.0 / total
    delta = delta * inverse
    dq = None
    lane = lax.broadcasted_iota(jnp.int32, (tq, HEAD), 1)
    low = lane < HEAD // 2
    for i in range(4):
        probs = scores[i] * inverse
        grad_low = (probs * (grad_probs[i] - delta)).astype(BF16)
        probs_low = probs.astype(BF16)
        dv = jnp.dot(probs_low, g, preferred_element_type=F32)
        dk = jnp.dot(grad_low, q, preferred_element_type=F32) * SCALE
        part = lax.dot_general(
            grad_low, keys_of(i), (((0,), (0,)), ((), ())), preferred_element_type=F32
        )
        dq = part if dq is None else dq + part
        if i == 3:
            grad_keys_ref[0] = dk.astype(BF16)
            grad_values_ref[0] = dv.astype(BF16)
        else:
            first = jnp.where(low, dk, pltpu.roll(dv, HEAD // 2, 1))
            second = jnp.where(low, pltpu.roll(dk, HEAD // 2, 1), dv)
            strips_ref[0, :, i] = first.astype(BF16).reshape(Y_CHIPS, tq // Y_CHIPS, HEAD)
            strips_ref[1, :, i] = second.astype(BF16).reshape(Y_CHIPS, tq // Y_CHIPS, HEAD)
    for h in range(group):
        grad_queries_ref[0, :, h * HEAD : (h + 1) * HEAD] = (
            dq[h * tq : (h + 1) * tq] * SCALE
        ).astype(BF16)


def reduce_kernel(
    z_chips,
    smp_size,
    where_ref,
    strips_ref,
    out_ref,
    held,
    part,
    sending,
    arriving,
    final,
    give_send,
    give_recv,
    own_sem,
    ring_send,
    ring_recv,
    last_send,
    last_recv,
):
    y, z, smp = place(z_chips)
    planes = Y_CHIPS * smp_size
    mine = y * smp_size + smp
    half = z_chips // 2
    enter(y, z, smp, z_chips, smp_size)

    def give(target, slot_send, slot_recv):
        py, ps = target
        return pltpu.make_async_remote_copy(
            src_ref=strips_ref.at[ps, py],
            dst_ref=held.at[pl.ds(3 * slot_recv, 3)],
            send_sem=give_send.at[slot_send],
            recv_sem=give_recv.at[slot_recv],
            device_id=(py * z_chips + z, ps),
            device_id_type=MESH,
        )

    def send(offset, carry):
        py, ps = peer_of(offset, y, smp, smp_size)
        give((py, ps), py * smp_size + ps, mine).start()
        return carry

    lax.fori_loop(1, planes, send, 0)
    keep = pltpu.make_async_copy(
        strips_ref.at[smp, y], held.at[pl.ds(3 * mine, 3)], own_sem.at[0]
    )
    keep.start()
    held[3 * planes] = jnp.zeros(held.shape[1:], BF16)

    def receive(offset, carry):
        sy, ss = source_of(offset, y, smp, smp_size)
        source = sy * smp_size + ss
        give((sy, ss), source, source).wait_recv()
        return carry

    lax.fori_loop(1, planes, receive, 0)
    keep.wait()

    def contribute(dest):
        def block(yb, carry):
            b = yb * z_chips + dest
            acc = held[where_ref[0, 0, b]].astype(F32)
            for k in range(1, planes):
                acc = acc + held[where_ref[k, 0, b]].astype(F32)
            part[yb] = acc
            return carry

        lax.fori_loop(0, Y_CHIPS, block, 0)

    def ring(way, step):
        to = (z + z_chips - 1) % z_chips if way == 0 else (z + 1) % z_chips
        return pltpu.make_async_remote_copy(
            src_ref=sending.at[way, step],
            dst_ref=arriving.at[way, step],
            send_sem=ring_send.at[way, step],
            recv_sem=ring_recv.at[way, step],
            device_id=(y * z_chips + to, smp),
            device_id_type=MESH,
        )

    def dest_of(way, step):
        far = half - step
        return (z + z_chips - far) % z_chips if way == 0 else (z + far) % z_chips

    def advance(way, step, first):
        contribute(dest_of(way, step))
        if first:
            sending[way, step] = part[...].astype(BF16)
        else:
            ring(way, step - 1).wait_recv()
            sending[way, step] = (part[...] + arriving[way, step - 1].astype(F32)).astype(BF16)
        ring(way, step).start()

    advance(0, 0, True)
    advance(1, 1, True)
    advance(0, 1, False)

    def both(step, carry):
        advance(1, step, False)
        advance(0, step, False)
        return carry

    lax.fori_loop(2, half, both, 0)
    contribute(z)
    for way in range(2):
        ring(way, half - 1).wait_recv()
    final[...] = (
        part[...]
        + arriving[0, half - 1].astype(F32)
        + arriving[1, half - 1].astype(F32)
    ).astype(BF16)

    rows = final.shape[1]

    def last(py, slot_recv):
        return pltpu.make_async_remote_copy(
            src_ref=final.at[py],
            dst_ref=out_ref.at[pl.ds(pl.multiple_of(slot_recv * rows, rows), rows)],
            send_sem=last_send.at[py],
            recv_sem=last_recv.at[slot_recv],
            device_id=(py * z_chips + z, smp),
            device_id_type=MESH,
        )

    for dy in range(1, Y_CHIPS):
        last((y + dy) % Y_CHIPS, y).start()
    out_ref[pl.ds(pl.multiple_of(y * rows, rows), rows)] = final[y]

    def finish(offset, carry):
        py, ps = peer_of(offset, y, smp, smp_size)
        give((py, ps), py * smp_size + ps, mine).wait_send()
        return carry

    lax.fori_loop(1, planes, finish, 0)
    for step in range(half):
        ring(0, step).wait_send()
        if step > 0:
            ring(1, step).wait_send()
    for dy in range(1, Y_CHIPS):
        last((y + dy) % Y_CHIPS, y).wait_send()
        py = (y + dy) % Y_CHIPS
        last(py, py).wait_recv()


def body(
    queries, out_grad, local_keys, trajectory_values, journal_keys, journal_values, picks, lengths
):
    smp_size = lax.axis_size("smp")
    z_chips = lax.axis_size("ctx") // Y_CHIPS
    planes = Y_CHIPS * smp_size
    block_rows, features = journal_keys.shape[1:]
    kv_heads = features // HEAD
    blocks = Y_CHIPS * z_chips
    rows = 2 * block_rows // planes
    cols = features // 2
    tq = queries.shape[1]
    wide = queries.shape[2] // kv_heads
    dma = pltpu.SemaphoreType.DMA
    any_space = pl.BlockSpec(memory_space=pl.ANY)
    in_smem = pl.BlockSpec(memory_space=pltpu.SMEM)
    in_vmem = pl.BlockSpec(memory_space=pltpu.VMEM)

    fetched, where = pl.pallas_call(
        functools.partial(fetch_kernel, z_chips, smp_size),
        out_shape=(
            jax.ShapeDtypeStruct((2, planes, 3, rows, cols), BF16),
            jax.ShapeDtypeStruct((planes, 1, 128), jnp.int32),
        ),
        in_specs=[in_smem, any_space, any_space],
        out_specs=(any_space, in_vmem),
        scratch_shapes=[
            pltpu.VMEM((2, blocks, rows, cols), BF16),
            pltpu.VMEM((2, planes, 3, rows, cols), BF16),
            pltpu.VMEM((planes, 1, 128), jnp.int32),
            pltpu.SMEM((planes, 1, 128), jnp.int32),
            dma((2, Y_CHIPS)),
            dma((2, Y_CHIPS)),
            dma((2,)),
            dma((planes,)),
            dma((planes,)),
            dma,
            dma((2, 2, z_chips // 2)),
            dma((2, z_chips)),
            dma((2, planes)),
            dma((2, planes)),
        ],
        compiler_params=pltpu.CompilerParams(
            collective_id=0, has_side_effects=True, vmem_limit_bytes=24 << 20
        ),
        name="fetch",
    )(picks, journal_keys, journal_values)

    head_wide = pl.BlockSpec((1, tq, wide), lambda g: (0, 0, g))
    head_narrow = pl.BlockSpec((1, tq, HEAD), lambda g: (0, 0, g))
    half_heads = kv_heads // 2
    grad_queries, grad_local_keys, grad_local_values, strips = pl.pallas_call(
        grads_kernel,
        grid=(kv_heads,),
        out_shape=(
            jax.ShapeDtypeStruct(queries.shape, BF16),
            jax.ShapeDtypeStruct(local_keys.shape, BF16),
            jax.ShapeDtypeStruct(local_keys.shape, BF16),
            jax.ShapeDtypeStruct((smp_size, Y_CHIPS, 3, tq // Y_CHIPS, HEAD), BF16),
        ),
        in_specs=[
            in_smem,
            head_wide,
            head_wide,
            head_narrow,
            head_narrow,
            pl.BlockSpec(
                (1, planes, 3, rows, HEAD), lambda g: (g // half_heads, 0, 0, 0, g % half_heads)
            ),
        ],
        out_specs=(
            head_wide,
            head_narrow,
            head_narrow,
            pl.BlockSpec((2, Y_CHIPS, 3, tq // Y_CHIPS, HEAD), lambda g: (g, 0, 0, 0, 0)),
        ),
        scratch_shapes=[
            pltpu.VMEM((4, tq, wide // HEAD * tq), F32),
            pltpu.VMEM((4, tq, wide // HEAD * tq), F32),
        ],
        compiler_params=pltpu.CompilerParams(vmem_limit_bytes=48 << 20),
        name="grads",
    )(lengths, queries, out_grad, local_keys, trajectory_values, fetched)

    piece = (tq // Y_CHIPS, HEAD)
    half = z_chips // 2
    summed = pl.pallas_call(
        functools.partial(reduce_kernel, z_chips, smp_size),
        out_shape=jax.ShapeDtypeStruct((block_rows, HEAD), BF16),
        in_specs=[in_smem, any_space],
        out_specs=in_vmem,
        scratch_shapes=[
            pltpu.VMEM((3 * planes + 1, *piece), BF16),
            pltpu.VMEM((Y_CHIPS, *piece), F32),
            pltpu.VMEM((2, half, Y_CHIPS, *piece), BF16),
            pltpu.VMEM((2, half, Y_CHIPS, *piece), BF16),
            pltpu.VMEM((Y_CHIPS, *piece), BF16),
            dma((planes,)),
            dma((planes,)),
            dma((1,)),
            dma((2, half)),
            dma((2, half)),
            dma((Y_CHIPS,)),
            dma((Y_CHIPS,)),
        ],
        compiler_params=pltpu.CompilerParams(
            collective_id=1, has_side_effects=True, vmem_limit_bytes=24 << 20
        ),
        name="reduce",
    )(where, strips)
    return (
        grad_queries,
        grad_local_keys,
        grad_local_values,
        summed[None, :, : HEAD // 2],
        summed[None, :, HEAD // 2 :],
    )


def solution(mesh):
    in_specs = (
        P("smp", "ctx", None),
        P("smp", "ctx", None),
        P("smp", "ctx", None),
        P("smp", "ctx", None),
        P("ctx", None, None),
        P("ctx", None, None),
        P("smp", "ctx", None),
        P("smp"),
    )
    out_specs = (
        P("smp", "ctx", None),
        P("smp", "ctx", None),
        P("smp", "ctx", None),
        P("ctx", None, "smp"),
        P("ctx", None, "smp"),
    )
    return jax.shard_map(body, mesh=mesh, in_specs=in_specs, out_specs=out_specs, check_vma=False)
```

time: 577 us -> 160 us (0.28)
  the two profiles are of different devices: /device:TPU:7 before, /device:TPU:36 now
where the time goes in v1:
time: 160 us; the launch traced here: 159 us
  Pallas kernels  150 us (94%)
  local copies, waits for them, and re-layouts  8.4 us (5%)
    pallas_call x1, Pallas kernels, body(): pl.pallas_call(functools.partial(reduce_kernel, z_chips, smp_size), out_s...  66.2 us
    pallas_call x1, Pallas kernels, body(): pl.pallas_call(functools.partial(fetch_kernel, z_chips, smp_size), out_sh...  62.5 us
    pallas_call x1, Pallas kernels, body(): pl.pallas_call(grads_kernel, grid=(kv_heads,), out_shape=(jax.ShapeDtypeS...  20.9 us
    unnamed x16, local copies, waits for them, and re-layouts  8.31 us

profile of v1, /device:TPU:36, one launch (start us, length us, event | category | flops | bytes accessed | tf_op | source)
XLA Modules:
  0.0 159.4 jit_solution(11416324756644206301)
XLA Ops:
  1.3 0.0 copy-start.4
  1.3 0.9 copy-done.4
  2.2 0.0 copy-start.5
  2.2 0.9 copy-done.5
  3.2 0.0 copy-start.6
  3.2 0.7 copy-done.6
  3.8 62.5 %fetch.1 = (bf16[2,32,3,16,256]{4,3,2,1,0:T(8,128)(2,1)S(1)}, s32[32,1,128]{2,1,0:T(1,128)S(1)}) custom-call(s32[1,1,3]{2,1,0:T(1,128)S(1)} %copy-done.6, bf16[1,256,512]{2,1,0:T(8,128)(2,1)S(1)} %copy-done.4, bf16[1,256,512]{2,1,0:T(8,128)(2,1)S(1)} %copy-done.5), custom_call_target="tpu_custom_call" | custom-call | tf_op jit(solution)/shard_map/fetch/pallas_call | solution.py:523
  66.4 0.0 copy-start
  66.4 1.2 copy-done
  67.6 0.0 copy-start.1
  67.6 1.2 copy-done.1
  68.8 0.0 copy-start.2
  68.8 0.9 copy-done.2
  69.8 0.0 copy-start.3
  69.8 0.9 copy-done.3
  70.7 20.9 %grads.1 = (bf16[1,256,2048]{2,1,0:T(8,128)(2,1)}, bf16[1,256,512]{2,1,0:T(8,128)(2,1)}, bf16[1,256,512]{2,1,0:T(8,128)(2,1)}, bf16[8,4,3,64,128]{4,3,2,1,0:T(8,128)(2,1)S(1)}) custom-call(s32[1]{0:T(128)S(6)} %copy.15.length_ref, bf16[1,256,2048]{2,1,0:T(8,128)(2,1)S(1)} %copy-done, bf16[1,256,2048]{2,1,0:T(8,128)(2,1)S(1)} %copy-done.1, ...), custom_call_target="tpu_custom_call" | custom-call | tf_op jit(solution)/shard_map/grads/pallas_call | solution.py:556
  91.6 66.2 %reduce.1 = bf16[256,128]{1,0:T(8,128)(2,1)S(1)} custom-call(s32[32,1,128]{2,1,0:T(1,128)S(1)} %get-tuple-element.15.where_ref, bf16[8,4,3,64,128]{4,3,2,1,0:T(8,128)(2,1)S(1)} %get-tuple-element.16.strips_ref), custom_call_target="tpu_custom_call" | custom-call | tf_op jit(solution)/shard_map/reduce/pallas_call | solution.py:591
  157.8 0.1 slice_bitcast_fusion
  157.9 0.7 copy.14
  158.6 0.7 copy.13
Async XLA Ops:
  1.3 1.0 copy-start.4
  2.2 0.9 copy-start.5
  3.2 0.7 copy-start.6
  66.4 1.2 copy-start
  67.6 1.2 copy-start.1
  68.8 0.9 copy-start.2
  69.8 0.9 copy-start.3

commit v2 on v0

v2 whole, which is shorter than its diff:
```python
import functools
import math

import jax
import jax.numpy as jnp
from jax import lax
from jax.experimental import pallas as pl
from jax.experimental.pallas import tpu as pltpu
from jax.sharding import PartitionSpec as P

HEAD = 128
Y_CHIPS = 4
SCALE = 1.0 / math.sqrt(HEAD)
CHUNKS = 2
TOP = 3
MESH = pl.DeviceIdType.MESH
BF16 = jnp.bfloat16
F32 = jnp.float32


def place(z_chips):
    ctx = lax.axis_index("ctx")
    return ctx // z_chips, ctx % z_chips, lax.axis_index("smp")


def peer_of(offset, y, smp, smp_size):
    half = smp_size // 2
    ds = offset % smp_size
    py = (y + offset // smp_size) % Y_CHIPS
    px = (smp // 2 + ds // 2) % half
    pc = (smp + ds) % 2
    return py, px * 2 + pc


def source_of(offset, y, smp, smp_size):
    half = smp_size // 2
    ds = offset % smp_size
    py = (y + Y_CHIPS - offset // smp_size) % Y_CHIPS
    px = (smp // 2 + half - ds // 2) % half
    pc = (smp + ds) % 2
    return py, px * 2 + pc


def enter(y, z, smp, z_chips, smp_size):
    barrier = pltpu.get_barrier_semaphore()
    count = Y_CHIPS * smp_size

    def greet(offset, carry):
        py, ps = peer_of(offset, y, smp, smp_size)
        pl.semaphore_signal(barrier, 1, device_id=(py * z_chips + z, ps), device_id_type=MESH)
        return carry

    for step in (1, z_chips - 1):
        pl.semaphore_signal(
            barrier,
            1,
            device_id=(y * z_chips + (z + step) % z_chips, smp),
            device_id_type=MESH,
        )
    lax.fori_loop(1, count, greet, 0)
    pl.semaphore_wait(barrier, count + 1)


def fused_kernel(
    z_chips,
    smp_size,
    picks_ref,
    length_ref,
    queries_ref,
    grad_ref,
    own_keys_ref,
    own_values_ref,
    keys_ref,
    values_ref,
    grad_queries_ref,
    grad_keys_ref,
    grad_values_ref,
    out_ref,
    log_0,
    log_1,
    staged,
    fetched,
    named,
    named_s,
    where_v,
    where_s,
    q_all,
    g_all,
    k_own,
    v_own,
    dq_all,
    dk_own,
    dv_own,
    scores,
    grad_probs,
    strips,
    held_0,
    held_1,
    part,
    sending,
    arriving,
    final,
    gathered,
    load_sem,
    store_sem,
    spread_send,
    spread_recv,
    own_sem,
    name_send,
    name_recv,
    smem_sem,
    ring_send,
    ring_recv,
    pick_send,
    pick_recv,
    give_send,
    give_recv,
    back_send,
    back_recv,
    last_send,
    last_recv,
):
    y, z, smp = place(z_chips)
    planes = Y_CHIPS * smp_size
    mine = y * smp_size + smp
    log = (log_0, log_1)
    held = (held_0, held_1)
    rows, cols = log_0.shape[1:]
    per_array = planes // 2
    half = z_chips // 2
    chunk_heads = cols // HEAD
    tq = q_all.shape[0]
    group = q_all.shape[1] // (CHUNKS * cols)
    width = group * tq
    lane = lax.broadcasted_iota(jnp.int32, (1, 128), 1)

    loads = [
        pltpu.make_async_copy(ref.at[0], scratch, load_sem.at[n])
        for n, (ref, scratch) in enumerate(
            (
                (queries_ref, q_all),
                (grad_ref, g_all),
                (own_keys_ref, k_own),
                (own_values_ref, v_own),
            )
        )
    ]
    named[mine] = jnp.where(
        lane == 0,
        picks_ref[0, 0, 0],
        jnp.where(lane == 1, picks_ref[0, 0, 1], picks_ref[0, 0, 2]),
    )
    enter(y, z, smp, z_chips, smp_size)

    def piece(ref, owner, c):
        row = pl.multiple_of((owner % per_array) * rows, rows)
        return ref.at[0, pl.ds(row, rows), pl.ds(c * cols, cols)]

    def spread(py, c, ref):
        return pltpu.make_async_remote_copy(
            src_ref=piece(ref, py * smp_size + smp, c),
            dst_ref=log[c].at[z * Y_CHIPS + y],
            send_sem=spread_send.at[c, py],
            recv_sem=spread_recv.at[c, y],
            device_id=(py * z_chips + z, smp),
            device_id_type=MESH,
        )

    def spread_in(py, c):
        return pltpu.make_async_remote_copy(
            src_ref=piece(keys_ref, mine, c),
            dst_ref=log[c].at[z * Y_CHIPS + py],
            send_sem=spread_send.at[c, py],
            recv_sem=spread_recv.at[c, py],
            device_id=(py * z_chips + z, smp),
            device_id_type=MESH,
        )

    def own(c, ref):
        return pltpu.make_async_copy(
            piece(ref, mine, c), log[c].at[z * Y_CHIPS + y], own_sem.at[c]
        )

    for c in range(CHUNKS):
        for dy in range(1, Y_CHIPS):
            py = (y + dy) % Y_CHIPS

            @pl.when(py < Y_CHIPS // 2)
            def _():
                spread(py, c, keys_ref).start()

            @pl.when(py >= Y_CHIPS // 2)
            def _():
                spread(py, c, values_ref).start()

        @pl.when(y < Y_CHIPS // 2)
        def _():
            own(c, keys_ref).start()

        @pl.when(y >= Y_CHIPS // 2)
        def _():
            own(c, values_ref).start()

    def name(target, slot_send, slot_recv):
        py, ps = target
        return pltpu.make_async_remote_copy(
            src_ref=named.at[mine],
            dst_ref=named.at[slot_recv],
            send_sem=name_send.at[slot_send],
            recv_sem=name_recv.at[slot_recv],
            device_id=(py * z_chips + z, ps),
            device_id_type=MESH,
        )

    def tell(offset, carry):
        py, ps = peer_of(offset, y, smp, smp_size)
        name((py, ps), py * smp_size + ps, mine).start()
        return carry

    lax.fori_loop(1, planes, tell, 0)
    for load in loads:
        load.start()

    def ring(c, way, step):
        slot = (z + z_chips - step) % z_chips if way == 0 else (z + step) % z_chips
        to = (z + 1) % z_chips if way == 0 else (z + z_chips - 1) % z_chips
        those = log[c].at[pl.ds(slot * Y_CHIPS, Y_CHIPS)]
        return pltpu.make_async_remote_copy(
            src_ref=those,
            dst_ref=those,
            send_sem=ring_send.at[c, way, min(step, half - 1)],
            recv_sem=ring_recv.at[c, slot],
            device_id=(y * z_chips + to, smp),
            device_id_type=MESH,
        )

    def ring_steps(c, way):
        return half if way == c % 2 else half - 1

    def begin(c):
        for dy in range(1, Y_CHIPS):
            spread_in((y + dy) % Y_CHIPS, c).wait_recv()
        own(c, keys_ref).wait()
        for way in range(2):
            ring(c, way, 0).start()

    def relay(c, step):
        for way in range(2):
            if step <= ring_steps(c, way):
                come = ring(c, way, step)
                come.wait_recv()
                if step < ring_steps(c, way):
                    come.start()

    def told(offset, carry):
        py, ps = source_of(offset, y, smp, smp_size)
        name((py, ps), py * smp_size + ps, py * smp_size + ps).wait_recv()
        return carry

    def locate(k, carry):
        found = jnp.full((1, 128), TOP * planes, jnp.int32)
        for i in range(TOP):
            found = jnp.where(lane == named_s[k, 0, i], TOP * k + i, found)
        where_v[k] = found
        return carry

    def give(c, target, slot_send, slot_recv):
        py, ps = target
        return pltpu.make_async_remote_copy(
            src_ref=staged.at[c, slot_send],
            dst_ref=fetched.at[c, slot_recv],
            send_sem=pick_send.at[c, slot_send],
            recv_sem=pick_recv.at[c, slot_recv],
            device_id=(py * z_chips + z, ps),
            device_id_type=MESH,
        )

    def place_of(target, i):
        block = named_s[target, 0, i]
        return (block % z_chips) * Y_CHIPS + block // z_chips

    def send_picks(c, first, end):
        def one(offset, carry):
            py, ps = peer_of(offset, y, smp, smp_size)
            target = py * smp_size + ps
            for i in range(TOP):
                staged[c, target, i] = log[c][place_of(target, i)]
            give(c, (py, ps), target, mine).start()
            return carry

        lax.fori_loop(first, end, one, 0)

    def keep_picks(c):
        for i in range(TOP):
            fetched[c, mine, i] = log[c][place_of(mine, i)]

    def take_picks(c):
        def one(offset, carry):
            py, ps = source_of(offset, y, smp, smp_size)
            source = py * smp_size + ps
            give(c, (py, ps), source, source).wait_recv()
            return carry

        lax.fori_loop(1, planes, one, 0)

    def grads(c):
        live_rows = length_ref[0] - lax.axis_index("ctx") * tq
        live = lax.broadcasted_iota(jnp.int32, (tq, HEAD), 0) < live_rows
        across = (((1,), (1,)), ((), ()))
        down = (((0,), (0,)), ((), ()))

        def one(n, carry):
            inner = pl.ds(pl.multiple_of(n * HEAD, HEAD), HEAD)
            lanes = pl.ds(pl.multiple_of(c * cols + n * HEAD, HEAD), HEAD)
            base = (c * chunk_heads + n) * group * HEAD
            wide = [pl.ds(pl.multiple_of(base + h * HEAD, HEAD), HEAD) for h in range(group)]
            q = jnp.concatenate([q_all[:, w] for w in wide], axis=0)
            raw = [g_all[:, w] for w in wide]
            g = jnp.concatenate([jnp.where(live, r, jnp.zeros_like(r)) for r in raw], axis=0)

            def keys_of(i):
                if i == TOP:
                    return k_own[:, lanes]
                return fetched[c, :per_array, i, :, inner].reshape(tq, HEAD)

            def values_of(i):
                if i == TOP:
                    return v_own[:, lanes]
                return fetched[c, per_array:, i, :, inner].reshape(tq, HEAD)

            top = None
            for i in range(TOP + 1):
                s = lax.dot_general(keys_of(i), q, across, preferred_element_type=F32)
                if i == TOP:
                    row = lax.broadcasted_iota(jnp.int32, (tq, width), 0)
                    col = lax.broadcasted_iota(jnp.int32, (tq, width), 1) % tq
                    s = jnp.where(col >= row, s, -1e30)
                scores[i] = s
                best = jnp.max(s, axis=0, keepdims=True)
                top = best if top is None else jnp.maximum(top, best)
                grad_probs[i] = lax.dot_general(
                    values_of(i), g, across, preferred_element_type=F32
                )
            total = jnp.zeros((1, width), F32)
            delta = jnp.zeros((1, width), F32)
            for i in range(TOP + 1):
                w = jnp.exp((scores[i] - top) * SCALE)
                scores[i] = w
                total = total + jnp.sum(w, axis=0, keepdims=True)
                delta = delta + jnp.sum(w * grad_probs[i], axis=0, keepdims=True)
            inverse = 1.0 / total
            delta = delta * inverse
            dq = None
            for i in range(TOP + 1):
                probs = scores[i] * inverse
                grad_low = (probs * (grad_probs[i] - delta)).astype(BF16)
                probs_low = probs.astype(BF16)
                dv = jnp.dot(probs_low, g, preferred_element_type=F32).astype(BF16)
                dk = jnp.dot(grad_low, q, preferred_element_type=F32) * SCALE
                dk = dk.astype(BF16)
                some = lax.dot_general(grad_low, keys_of(i), down, preferred_element_type=F32)
                dq = some if dq is None else dq + some
                if i == TOP:
                    dk_own[:, lanes] = dk
                    dv_own[:, lanes] = dv
                else:
                    strips[c, :per_array, i, :, inner] = dk.reshape(per_array, rows, HEAD)
                    strips[c, per_array:, i, :, inner] = dv.reshape(per_array, rows, HEAD)
            for h in range(group):
                dq_all[:, wide[h]] = (dq[h * tq : (h + 1) * tq] * SCALE).astype(BF16)
            return carry

        lax.fori_loop(0, chunk_heads, one, 0)

    def back(c, target, slot_send, slot_recv):
        py, ps = target
        return pltpu.make_async_remote_copy(
            src_ref=strips.at[c, slot_send],
            dst_ref=held[c].at[pl.ds(TOP * slot_recv, TOP)],
            send_sem=give_send.at[c, slot_send],
            recv_sem=give_recv.at[c, slot_recv],
            device_id=(py * z_chips + z, ps),
            device_id_type=MESH,
        )

    def send_partials(c):
        def one(offset, carry):
            py, ps = peer_of(offset, y, smp, smp_size)
            back(c, (py, ps), py * smp_size + ps, mine).start()
            return carry

        lax.fori_loop(1, planes, one, 0)
        for i in range(TOP):
            held[c][TOP * mine + i] = strips[c, mine, i]

    def take_partials(c):
        def one(offset, carry):
            py, ps = source_of(offset, y, smp, smp_size)
            source = py * smp_size + ps
            back(c, (py, ps), source, source).wait_recv()
            return carry

        lax.fori_loop(1, planes, one, 0)

    def contribute(c, way, dest):
        def block(yb, carry):
            b = yb * z_chips + dest
            acc = held[c][where_s[0, 0, b]].astype(F32)
            for k in range(1, planes):
                acc = acc + held[c][where_s[k, 0, b]].astype(F32)
            part[way, yb] = acc
            return carry

        lax.fori_loop(0, Y_CHIPS, block, 0)

    def ring_back(c, way, step):
        to = (z + z_chips - 1) % z_chips if way == 0 else (z + 1) % z_chips
        return pltpu.make_async_remote_copy(
            src_ref=sending.at[c, way, step],
            dst_ref=arriving.at[c, way, step],
            send_sem=back_send.at[c, way, step],
            recv_sem=back_recv.at[c, way, step],
            device_id=(y * z_chips + to, smp),
            device_id_type=MESH,
        )

    def first_step(c, way):
        return 0 if way == c % 2 else 1

    def relay_back(c, step):
        ways = [way for way in range(2) if step >= first_step(c, way)]
        for way in ways:
            far = half - step
            contribute(
                c, way, (z + z_chips - far) % z_chips if way == 0 else (z + far) % z_chips
            )
        for way in ways:
            if step == first_step(c, way):
                sending[c, way, step] = part[way].astype(BF16)
            else:
                ring_back(c, way, step - 1).wait_recv()
                sending[c, way, step] = (
                    part[way] + arriving[c, way, step - 1].astype(F32)
                ).astype(BF16)
            ring_back(c, way, step).start()

    def last(c, py, ps, slot_send, slot_recv):
        return pltpu.make_async_remote_copy(
            src_ref=final.at[c, (ps // 2) % chunk_heads, py],
            dst_ref=gathered.at[slot_recv],
            send_sem=last_send.at[slot_send],
            recv_sem=last_recv.at[slot_recv],
            device_id=(py * z_chips + z, ps),
            device_id_type=MESH,
        )

    owners = smp_size // CHUNKS

    def owner_of(c, n):
        return (y + n // owners) % Y_CHIPS, c * owners + (smp + n) % owners

    def close(c):
        contribute(c, 0, z)
        for way in range(2):
            ring_back(c, way, half - 1).wait_recv()
        whole = (
            part[0]
            + arriving[c, 0, half - 1].astype(F32)
            + arriving[c, 1, half - 1].astype(F32)
        ).astype(BF16)
        for n in range(chunk_heads):
            final[c, n] = whole[:, :, n * HEAD : (n + 1) * HEAD]

        def one(n, carry):
            py, ps = owner_of(c, n)
            target = py * smp_size + ps

            @pl.when(target != mine)
            def _():
                last(c, py, ps, target, mine).start()

            return carry

        lax.fori_loop(0, Y_CHIPS * owners, one, 0)

    def stores(c):
        narrow = pl.ds(c * cols, cols)
        wide = pl.ds(c * cols * group, cols * group)
        return [
            pltpu.make_async_copy(
                scratch.at[:, part_of], ref.at[0, :, part_of], store_sem.at[c, n]
            )
            for n, (scratch, ref, part_of) in enumerate(
                (
                    (dq_all, grad_queries_ref, wide),
                    (dk_own, grad_keys_ref, narrow),
                    (dv_own, grad_values_ref, narrow),
                )
            )
        ]

    lag = 2
    begin(0)
    begin(1)
    lax.fori_loop(1, planes, told, 0)
    to_smem = pltpu.make_async_copy(named, named_s, smem_sem.at[0])
    to_smem.start()
    for step in range(1, half + 1):
        relay(0, step)
        if step > lag:
            relay(1, step - lag)
        if step == 1:
            to_smem.wait()
    lead = planes // (lag + 1)
    send_picks(0, 1, lead)
    for n in range(lag):
        relay(1, half - lag + 1 + n)
        send_picks(0, lead * (n + 1), planes if n == lag - 1 else lead * (n + 2))
    keep_picks(0)
    send_picks(1, 1, planes)
    keep_picks(1)
    lax.fori_loop(0, planes, locate, 0)
    where_copy = pltpu.make_async_copy(where_v, where_s, smem_sem.at[1])
    where_copy.start()
    for c in range(CHUNKS):
        held[c][TOP * planes] = jnp.zeros((rows, cols), BF16)
    for load in loads:
        load.wait()
    take_picks(0)
    grads(0)
    send_partials(0)
    for copy in stores(0):
        copy.start()
    take_picks(1)
    grads(1)
    send_partials(1)
    for copy in stores(1):
        copy.start()
    where_copy.wait()
    take_partials(0)
    back_lag = 3
    for step in range(half + back_lag):
        if step < half:
            relay_back(0, step)
        if step == half:
            close(0)
        if step == back_lag:
            take_partials(1)
        if step >= back_lag:
            relay_back(1, step - back_lag)
    close(1)

    for c in range(CHUNKS):
        @pl.when(smp // owners == c)
        def _():
            gathered[mine] = final[c, (smp // 2) % chunk_heads, y]

    def take_last(offset, carry):
        sy, ss = source_of(offset, y, smp, smp_size)
        source = sy * smp_size + ss
        last(0, sy, ss, source, source).wait_recv()
        return carry

    lax.fori_loop(1, planes, take_last, 0)
    got_keys = gathered[:per_array].reshape(per_array * rows, HEAD)
    got_values = gathered[per_array:].reshape(per_array * rows, HEAD)
    low = lax.broadcasted_iota(jnp.int32, got_keys.shape, 1) < HEAD // 2
    got_keys = got_keys.astype(F32)
    got_values = got_values.astype(F32)
    even = jnp.where(low, got_keys, pltpu.roll(got_values, HEAD // 2, 1))
    odd = jnp.where(low, pltpu.roll(got_keys, HEAD // 2, 1), got_values)
    out_ref[...] = jnp.where(smp % 2 == 0, even, odd).astype(BF16)

    for c in range(CHUNKS):
        for dy in range(1, Y_CHIPS):
            spread((y + dy) % Y_CHIPS, c, keys_ref).wait_send()
        for way in range(2):
            for step in range(ring_steps(c, way)):
                ring(c, way, step).wait_send()
            for step in range(first_step(c, way), half):
                ring_back(c, way, step).wait_send()
        for copy in stores(c):
            copy.wait()

    def finish(offset, carry):
        py, ps = peer_of(offset, y, smp, smp_size)
        target = py * smp_size + ps
        name((py, ps), target, mine).wait_send()
        for c in range(CHUNKS):
            give(c, (py, ps), target, mine).wait_send()
            back(c, (py, ps), target, mine).wait_send()
        last(0, py, ps, target, mine).wait_send()
        return carry

    lax.fori_loop(1, planes, finish, 0)


def body(
    queries, out_grad, local_keys, trajectory_values, journal_keys, journal_values, picks, lengths
):
    smp_size = lax.axis_size("smp")
    z_chips = lax.axis_size("ctx") // Y_CHIPS
    planes = Y_CHIPS * smp_size
    block_rows, features = journal_keys.shape[1:]
    blocks = Y_CHIPS * z_chips
    rows = 2 * block_rows // planes
    cols = features // CHUNKS
    tq = queries.shape[1]
    width = queries.shape[2] // (features // HEAD) // HEAD * tq
    half = z_chips // 2
    heads = cols // HEAD
    dma = pltpu.SemaphoreType.DMA
    vmem = pltpu.VMEM
    any_space = pl.BlockSpec(memory_space=pl.ANY)
    in_smem = pl.BlockSpec(memory_space=pltpu.SMEM)
    in_vmem = pl.BlockSpec(memory_space=pltpu.VMEM)
    grad_queries, grad_local_keys, grad_local_values, summed = pl.pallas_call(
        functools.partial(fused_kernel, z_chips, smp_size),
        out_shape=(
            jax.ShapeDtypeStruct(queries.shape, BF16),
            jax.ShapeDtypeStruct(local_keys.shape, BF16),
            jax.ShapeDtypeStruct(local_keys.shape, BF16),
            jax.ShapeDtypeStruct((block_rows, HEAD), BF16),
        ),
        in_specs=[in_smem, in_smem] + [any_space] * 6,
        out_specs=(any_space, any_space, any_space, in_vmem),
        scratch_shapes=[
            vmem((blocks, rows, cols), BF16),
            vmem((blocks, rows, cols), BF16),
            vmem((CHUNKS, planes, TOP, rows, cols), BF16),
            vmem((CHUNKS, planes, TOP, rows, cols), BF16),
            vmem((planes, 1, 128), jnp.int32),
            pltpu.SMEM((planes, 1, 128), jnp.int32),
            vmem((planes, 1, 128), jnp.int32),
            pltpu.SMEM((planes, 1, 128), jnp.int32),
            vmem(queries.shape[1:], BF16),
            vmem(queries.shape[1:], BF16),
            vmem(local_keys.shape[1:], BF16),
            vmem(local_keys.shape[1:], BF16),
            vmem(queries.shape[1:], BF16),
            vmem(local_keys.shape[1:], BF16),
            vmem(local_keys.shape[1:], BF16),
            vmem((TOP + 1, tq, width), F32),
            vmem((TOP + 1, tq, width), F32),
            vmem((CHUNKS, planes, TOP, rows, cols), BF16),
            vmem((TOP * planes + 1, rows, cols), BF16),
            vmem((TOP * planes + 1, rows, cols), BF16),
            vmem((2, Y_CHIPS, rows, cols), F32),
            vmem((CHUNKS, 2, half, Y_CHIPS, rows, cols), BF16),
            vmem((CHUNKS, 2, half, Y_CHIPS, rows, cols), BF16),
            vmem((CHUNKS, heads, Y_CHIPS, rows, HEAD), BF16),
            vmem((planes, rows, HEAD), BF16),
            dma((4,)),
            dma((CHUNKS, 3)),
            dma((CHUNKS, Y_CHIPS)),
            dma((CHUNKS, Y_CHIPS)),
            dma((CHUNKS,)),
            dma((planes,)),
            dma((planes,)),
            dma((2,)),
            dma((CHUNKS, 2, half)),
            dma((CHUNKS, z_chips)),
            dma((CHUNKS, planes)),
            dma((CHUNKS, planes)),
            dma((CHUNKS, planes)),
            dma((CHUNKS, planes)),
            dma((CHUNKS, 2, half)),
            dma((CHUNKS, 2, half)),
            dma((planes,)),
            dma((planes,)),
        ],
        compiler_params=pltpu.CompilerParams(
            collective_id=0, has_side_effects=True, vmem_limit_bytes=56 << 20
        ),
        name="sparse_attention_grads",
    )(
        picks,
        lengths,
        queries,
        out_grad,
        local_keys,
        trajectory_values,
        journal_keys,
        journal_values,
    )
    return (
        grad_queries,
        grad_local_keys,
        grad_local_values,
        summed[None, :, : HEAD // 2],
        summed[None, :, HEAD // 2 :],
    )


def solution(mesh):
    in_specs = (
        P("smp", "ctx", None),
        P("smp", "ctx", None),
        P("smp", "ctx", None),
        P("smp", "ctx", None),
        P("ctx", None, None),
        P("ctx", None, None),
        P("smp", "ctx", None),
        P("smp"),
    )
    out_specs = (
        P("smp", "ctx", None),
        P("smp", "ctx", None),
        P("smp", "ctx", None),
        P("ctx", None, "smp"),
        P("ctx", None, "smp"),
    )
    return jax.shard_map(body, mesh=mesh, in_specs=in_specs, out_specs=out_specs, check_vma=False)
```

time: 577 us -> 142 us (0.25)
  waiting for transfers between devices: 202 us -> 0 us
  blocking collectives: 183 us -> 0 us
  Pallas kernels: 0 us -> 134 us
  starting transfers between devices: 79.3 us -> 0 us
  matrix products: 49.8 us -> 0 us
  local copies, waits for them, and re-layouts: 44.7 us -> 6.52 us
  other arithmetic: 12.8 us -> 0 us
    all_to_all x8 -> x0, waiting for transfers between devices: 202 us -> none  [the longest x1 53.2 us: body(): lax.all_to_all(log_key_grad, 'ctx', split_axis=1, concat_axis=1, tiled=True)]
    pallas_call x0 -> x1, Pallas kernels: none -> 134 us  [body(): pl.pallas_call(functools.partial(fused_kernel, z_chips, smp_size), out_sh...]
    unnamed x1 -> x0, blocking collectives: 117 us -> none
    all_to_all x8 -> x0, starting transfers between devices: 79.3 us -> none  [the longest x1 18.5 us: body(): lax.all_to_all(journal_values.reshape(1, ctx_size, piece_rows, feature_ax...]
    all_gather x1 -> x0, blocking collectives: 65.6 us -> none  [body(): wanted = lax.all_gather(picks[0], 'ctx', axis=0, tiled=True)]
    dot_general x22 -> x0, matrix products: 31.8 us -> none  [the longest x4 10.7 us: head_grads(): jnp.einsum('gtk,tgd->kd', grad_low, query_head, preferred_element_type=jn...]
    sub x4 -> x0, matrix products: 18 us -> none  [head_grads(): weights = jnp.exp(scores - top_score)]
    reshape x6 -> x0, local copies, waits for them, and re-layouts: 10.7 us -> none  [the longest x2 4.96 us: body(): key_gradient[:split_row]]
  transfers between devices with their start and end apart: 8 -> 0, of which waited for: 7 -> 0; matrix products, arithmetic and copies ran while one was open for 6% -> 0% of each run, Pallas kernels for 0% -> 0%
where the time goes in v2:
time: 142 us
  Pallas kernels  134 us (94%)
  local copies, waits for them, and re-layouts  6.52 us (5%)
    pallas_call x1, Pallas kernels, body(): pl.pallas_call(functools.partial(fused_kernel, z_chips, smp_size), out_sh...  134 us
    unnamed x9, local copies, waits for them, and re-layouts  5.52 us

profile of v2, /device:TPU:7, one launch (start us, length us, event | category | flops | bytes accessed | tf_op | source)
XLA Modules:
  0.0 142.2 jit_solution(15559477157846888325)
XLA Ops:
  1.3 134.4 %sparse_attention_grads.1 = (bf16[1,256,2048]{2,1,0:T(8,128)(2,1)}, bf16[1,256,512]{2,1,0:T(8,128)(2,1)}, bf16[1,256,512]{2,1,0:T(8,128)(2,1)}, bf16[256,128]{1,0:T(8,128)(2,1)}) custom-call(s32[1,1,3]{2,1,0:T(1,128)} %picks_ref.1, s32[1]{0:T(128)S(6)} %copy.18.length_ref, bf16[1,256,2048]{2,1,0:T(8,128)(2,1)} %queries_ref.1, ...), custom_call_target="tpu_custom_call" | custom-call | tf_op jit(solution)/shard_map/sparse_attention_grads/pallas_call | solution.py:617
  135.7 1.0 slice_bitcast_fusion
  136.7 0.7 copy.14
  137.4 0.7 copy.13
  138.1 0.0 copy-start.1
  138.1 2.3 %copy.19 = bf16[1,256,2048]{2,1,0:T(8,128)(2,1)} copy(bf16[1,256,2048]{2,1,0:T(8,128)(2,1)} %get-tuple-element.25) | data formatting | bytes 2097152
  140.4 0.0 copy-done.1
  140.4 0.0 copy-start
  140.4 0.7 copy.20
  141.1 0.3 copy-done
  141.5 0.7 copy.21
Async XLA Ops:
  138.1 2.4 %copy-start.1 = (bf16[1,256,512]{2,1,0:T(8,128)(2,1)S(1)}, bf16[1,256,512]{2,1,0:T(8,128)(2,1)}, u32[]{:S(2)}) copy-start(bf16[1,256,512]{2,1,0:T(8,128)(2,1)} %get-tuple-element.26) | copy-start | bytes 786436
  140.4 1.0 copy-start

commit v3 on v2

v3 whole, which is shorter than its diff:
```python
import functools
import math

import jax
import jax.numpy as jnp
from jax import lax
from jax.experimental import pallas as pl
from jax.experimental.pallas import tpu as pltpu
from jax.sharding import PartitionSpec as P

HEAD = 128
Y_CHIPS = 4
SCALE = 1.0 / math.sqrt(HEAD)
CHUNKS = 2
TOP = 3
MESH = pl.DeviceIdType.MESH
BF16 = jnp.bfloat16
F32 = jnp.float32


def place(z_chips):
    ctx = lax.axis_index("ctx")
    return ctx // z_chips, ctx % z_chips, lax.axis_index("smp")


def plane_of(y, z, smp, z_chips, smp_size):
    xs = smp_size // 2
    x, core = smp // 2, lax.rem(smp, 2)
    along_y = [lax.rem(y + d, Y_CHIPS) for d in range(Y_CHIPS)]
    along_smp = [
        lax.rem(x + d // 2, xs) * 2 + lax.rem(core + d % 2, 2) for d in range(smp_size)
    ]
    peers = []
    for dy in range(Y_CHIPS):
        for ds in range(smp_size):
            if dy + ds > 0:
                peers.append(
                    (
                        (along_y[dy] * z_chips + z, along_smp[ds]),
                        along_y[dy] * smp_size + along_smp[ds],
                    )
                )
    return peers


def enter(y, z, smp, z_chips, peers):
    barrier = pltpu.get_barrier_semaphore()
    near = [(y * z_chips + lax.rem(z + d, z_chips), smp) for d in along_z(z_chips)]
    for device in near + [device for device, _ in peers]:
        pl.semaphore_signal(barrier, 1, device_id=device, device_id_type=MESH)
    pl.semaphore_wait(barrier, len(near) + len(peers))


def along_z(z_chips):
    return [d % z_chips for d in (1, -1, 2, -2, 3, -3)]


def eight(c):
    return 1 if c % 2 == 0 else -1


def down_tree(c):
    sends = [(0, 3), (0, -3), (0, 1), (0, -1)]
    for side in (1, -1):
        sends += [(3 * side, 3 * side), (3 * side, side), (3 * side, -side)]
    for side in (1, -1):
        sends += [(6 * side, side), (6 * side, -side)]
    return sends + [(6 * eight(c), 2 * eight(c))]


UP_LEAVES = (5, 7, 2, 4, 1)
UP = {1: -1, 2: 1, 3: -3, 4: -1, 5: 1, 6: -3, 7: -1, 8: -2}


def up_tree(c):
    roles = [(r * side, UP[r] * side) for r in range(1, 8) for side in (1, -1)]
    return roles + [(8 * eight(c), UP[8] * eight(c))]


def fused_kernel(
    z_chips,
    smp_size,
    picks_ref,
    length_ref,
    queries_ref,
    grad_ref,
    own_keys_ref,
    own_values_ref,
    keys_ref,
    values_ref,
    grad_queries_ref,
    grad_keys_ref,
    grad_values_ref,
    out_ref,
    log_0,
    log_1,
    staged,
    fetched,
    named,
    named_s,
    where_v,
    where_s,
    q_all,
    g_all,
    k_own,
    v_own,
    dq_all,
    dk_own,
    dv_own,
    scores,
    grad_probs,
    strips,
    held_0,
    held_1,
    sending,
    arriving,
    final,
    gathered,
    load_sem,
    store_sem,
    spread_send,
    spread_recv,
    own_sem,
    name_send,
    name_recv,
    smem_sem,
    ring_send,
    ring_recv,
    pick_send,
    pick_recv,
    give_send,
    give_recv,
    back_send,
    back_recv,
    last_send,
    last_recv,
):
    y, z, smp = place(z_chips)
    planes = Y_CHIPS * smp_size
    mine = y * smp_size + smp
    peers = plane_of(y, z, smp, z_chips, smp_size)
    others = planes - 1
    log = (log_0, log_1)
    held = (held_0, held_1)
    rows, cols = log_0.shape[1:]
    per_array = planes // 2
    chunk_heads = cols // HEAD
    tq = q_all.shape[0]
    group = q_all.shape[1] // (CHUNKS * cols)
    width = group * tq
    lane = lax.broadcasted_iota(jnp.int32, (1, 128), 1)

    loads = [
        pltpu.make_async_copy(ref.at[0], scratch, load_sem.at[n])
        for n, (ref, scratch) in enumerate(
            (
                (queries_ref, q_all),
                (grad_ref, g_all),
                (own_keys_ref, k_own),
                (own_values_ref, v_own),
            )
        )
    ]
    named[mine] = jnp.where(
        lane == 0,
        picks_ref[0, 0, 0],
        jnp.where(lane == 1, picks_ref[0, 0, 1], picks_ref[0, 0, 2]),
    )
    enter(y, z, smp, z_chips, peers)

    def piece(ref, owner, c):
        row = pl.multiple_of((owner % per_array) * rows, rows)
        return ref.at[0, pl.ds(row, rows), pl.ds(c * cols, cols)]

    def spread(py, c, ref):
        return pltpu.make_async_remote_copy(
            src_ref=piece(ref, py * smp_size + smp, c),
            dst_ref=log[c].at[z * Y_CHIPS + y],
            send_sem=spread_send.at[c, py],
            recv_sem=spread_recv.at[c, y],
            device_id=(py * z_chips + z, smp),
            device_id_type=MESH,
        )

    def spread_in(py, c):
        return pltpu.make_async_remote_copy(
            src_ref=piece(keys_ref, mine, c),
            dst_ref=log[c].at[z * Y_CHIPS + py],
            send_sem=spread_send.at[c, py],
            recv_sem=spread_recv.at[c, py],
            device_id=(py * z_chips + z, smp),
            device_id_type=MESH,
        )

    def own(c, ref):
        return pltpu.make_async_copy(
            piece(ref, mine, c), log[c].at[z * Y_CHIPS + y], own_sem.at[c]
        )

    for c in range(CHUNKS):
        for dy in range(1, Y_CHIPS):
            py = (y + dy) % Y_CHIPS

            @pl.when(py < Y_CHIPS // 2)
            def _():
                spread(py, c, keys_ref).start()

            @pl.when(py >= Y_CHIPS // 2)
            def _():
                spread(py, c, values_ref).start()

        @pl.when(y < Y_CHIPS // 2)
        def _():
            own(c, keys_ref).start()

        @pl.when(y >= Y_CHIPS // 2)
        def _():
            own(c, values_ref).start()

    def name(device, slots):
        return pltpu.make_async_remote_copy(
            src_ref=named.at[mine] if slots is None else named.at[slots],
            dst_ref=named.at[mine] if slots is None else named.at[slots],
            send_sem=name_send.at[0],
            recv_sem=name_recv.at[0],
            device_id=device,
            device_id_type=MESH,
        )

    one_peer = peers[0][0]
    for device, _ in peers:
        name(device, None).start()
    for load in loads:
        load.start()

    def pass_on(c, source, step):
        slot = lax.rem(z + (z_chips - source) % z_chips, z_chips)
        to = lax.rem(z + step % z_chips, z_chips)
        those = log[c].at[pl.ds(slot * Y_CHIPS, Y_CHIPS)]
        return pltpu.make_async_remote_copy(
            src_ref=those,
            dst_ref=those,
            send_sem=ring_send.at[c, down_tree(c).index((source, step))],
            recv_sem=ring_recv.at[c, slot],
            device_id=(y * z_chips + to, smp),
            device_id_type=MESH,
        )

    def arrived(c, source):
        slot = lax.rem(z + (z_chips - source) % z_chips, z_chips)
        those = log[c].at[pl.ds(slot * Y_CHIPS, Y_CHIPS)]
        pltpu.make_async_remote_copy(
            src_ref=those,
            dst_ref=those,
            send_sem=ring_send.at[c, 0],
            recv_sem=ring_recv.at[c, slot],
            device_id=one_peer,
            device_id_type=MESH,
        ).wait_recv()

    def begin(c):
        for dy in range(1, Y_CHIPS):
            spread_in((y + dy) % Y_CHIPS, c).wait_recv()
        own(c, keys_ref).wait()
        relay(c, 0)

    def relay(c, distance):
        for side in (1, -1) if distance else (1,):
            source = distance * side
            if distance:
                arrived(c, source)
            for start, step in down_tree(c):
                if start == source:
                    pass_on(c, start, step).start()

    def leaves(c):
        for distance in (1, 2, 4, 5, 7):
            for side in (1, -1):
                arrived(c, distance * side)
        arrived(c, 8 * eight(c))

    def locate(k, carry):
        found = jnp.full((1, 128), TOP * planes, jnp.int32)
        for i in range(TOP):
            found = jnp.where(lane == named_s[k, 0, i], TOP * k + i, found)
        where_v[k] = found
        return carry

    def give(c, device, slot_send, slot_recv):
        return pltpu.make_async_remote_copy(
            src_ref=staged.at[c, slot_send],
            dst_ref=fetched.at[c, slot_recv],
            send_sem=pick_send.at[c],
            recv_sem=pick_recv.at[c],
            device_id=device,
            device_id_type=MESH,
        )

    def place_of(target, i):
        block = named_s[target, 0, i]
        return lax.rem(block, z_chips) * Y_CHIPS + lax.div(block, z_chips)

    def send_picks(c, some):
        for device, target in some:
            for i in range(TOP):
                staged[c, target, i] = log[c][place_of(target, i)]
            give(c, device, target, mine).start()

    def keep_picks(c):
        for i in range(TOP):
            fetched[c, mine, i] = log[c][place_of(mine, i)]

    def all_picks(c):
        return give(c, one_peer, pl.ds(0, others), pl.ds(0, others))

    def grads(c):
        live_rows = length_ref[0] - lax.axis_index("ctx") * tq
        live = lax.broadcasted_iota(jnp.int32, (tq, HEAD), 0) < live_rows
        across = (((1,), (1,)), ((), ()))
        down = (((0,), (0,)), ((), ()))

        def one(n, carry):
            inner = pl.ds(pl.multiple_of(n * HEAD, HEAD), HEAD)
            lanes = pl.ds(pl.multiple_of(c * cols + n * HEAD, HEAD), HEAD)
            base = (c * chunk_heads + n) * group * HEAD
            wide = [pl.ds(pl.multiple_of(base + h * HEAD, HEAD), HEAD) for h in range(group)]
            q = jnp.concatenate([q_all[:, w] for w in wide], axis=0)
            raw = [g_all[:, w] for w in wide]
            g = jnp.concatenate([jnp.where(live, r, jnp.zeros_like(r)) for r in raw], axis=0)

            def keys_of(i):
                if i == TOP:
                    return k_own[:, lanes]
                return fetched[c, :per_array, i, :, inner].reshape(tq, HEAD)

            def values_of(i):
                if i == TOP:
                    return v_own[:, lanes]
                return fetched[c, per_array:, i, :, inner].reshape(tq, HEAD)

            top = None
            for i in range(TOP + 1):
                s = lax.dot_general(keys_of(i), q, across, preferred_element_type=F32)
                if i == TOP:
                    row = lax.broadcasted_iota(jnp.int32, (tq, width), 0)
                    col = lax.broadcasted_iota(jnp.int32, (tq, width), 1) % tq
                    s = jnp.where(col >= row, s, -1e30)
                scores[i] = s
                best = jnp.max(s, axis=0, keepdims=True)
                top = best if top is None else jnp.maximum(top, best)
                grad_probs[i] = lax.dot_general(
                    values_of(i), g, across, preferred_element_type=F32
                )
            total = jnp.zeros((1, width), F32)
            delta = jnp.zeros((1, width), F32)
            for i in range(TOP + 1):
                w = jnp.exp((scores[i] - top) * SCALE)
                scores[i] = w
                total = total + jnp.sum(w, axis=0, keepdims=True)
                delta = delta + jnp.sum(w * grad_probs[i], axis=0, keepdims=True)
            inverse = 1.0 / total
            delta = delta * inverse
            dq = None
            for i in range(TOP + 1):
                probs = scores[i] * inverse
                grad_low = (probs * (grad_probs[i] - delta)).astype(BF16)
                probs_low = probs.astype(BF16)
                dv = jnp.dot(probs_low, g, preferred_element_type=F32).astype(BF16)
                dk = jnp.dot(grad_low, q, preferred_element_type=F32) * SCALE
                dk = dk.astype(BF16)
                some = lax.dot_general(grad_low, keys_of(i), down, preferred_element_type=F32)
                dq = some if dq is None else dq + some
                if i == TOP:
                    dk_own[:, lanes] = dk
                    dv_own[:, lanes] = dv
                else:
                    strips[c, :per_array, i, :, inner] = dk.reshape(per_array, rows, HEAD)
                    strips[c, per_array:, i, :, inner] = dv.reshape(per_array, rows, HEAD)
            for h in range(group):
                dq_all[:, wide[h]] = (dq[h * tq : (h + 1) * tq] * SCALE).astype(BF16)
            return carry

        lax.fori_loop(0, chunk_heads, one, 0)

    def back(c, device, slot_send, slot_recv):
        return pltpu.make_async_remote_copy(
            src_ref=strips.at[c, slot_send],
            dst_ref=held[c].at[slot_recv],
            send_sem=give_send.at[c],
            recv_sem=give_recv.at[c],
            device_id=device,
            device_id_type=MESH,
        )

    def send_partials(c):
        for device, target in peers:
            back(c, device, target, pl.ds(TOP * mine, TOP)).start()
        for i in range(TOP):
            held[c][TOP * mine + i] = strips[c, mine, i]

    def all_partials(c):
        return pltpu.make_async_remote_copy(
            src_ref=held[c].at[pl.ds(0, TOP * others)],
            dst_ref=held[c].at[pl.ds(0, TOP * others)],
            send_sem=give_send.at[c],
            recv_sem=give_recv.at[c],
            device_id=one_peer,
            device_id_type=MESH,
        )

    def total_of(c, role, yb, feeders):
        b = yb * z_chips + lax.rem(z + (z_chips - role) % z_chips, z_chips)
        acc = held[c][where_s[0, 0, b]].astype(F32)
        for k in range(1, planes):
            acc = acc + held[c][where_s[k, 0, b]].astype(F32)
        for feeder in feeders:
            acc = acc + arriving[c, slot_of(c, feeder), yb].astype(F32)
        return acc

    def slot_of(c, role):
        return [r for r, _ in up_tree(c)].index(role)

    def pass_up(c, role):
        slot = slot_of(c, role)
        to = lax.rem(z + up_tree(c)[slot][1] % z_chips, z_chips)
        return pltpu.make_async_remote_copy(
            src_ref=sending.at[c, slot],
            dst_ref=arriving.at[c, slot],
            send_sem=back_send.at[c, slot],
            recv_sem=back_recv.at[c, slot],
            device_id=(y * z_chips + to, smp),
            device_id_type=MESH,
        )

    def feeders_of(c, role):
        side = 1 if role > 0 else -1
        if abs(role) == 3:
            return [2 * side, 4 * side, 6 * side]
        if abs(role) == 6:
            return [5 * side, 7 * side] + ([8 * side] if side == eight(c) else [])
        return [1, -1, 3, -3] if role == 0 else []

    def send_up(c, role):
        feeders = feeders_of(c, role)
        slot = slot_of(c, role)
        for feeder in feeders:
            pass_up(c, feeder).wait_recv()

        def block(yb, carry):
            sending[c, slot, yb] = total_of(c, role, yb, feeders).astype(BF16)
            return carry

        lax.fori_loop(0, Y_CHIPS, block, 0)
        pass_up(c, role).start()

    def last(c, device, head, py, slot_recv):
        return pltpu.make_async_remote_copy(
            src_ref=final.at[c, head, py],
            dst_ref=gathered.at[slot_recv],
            send_sem=last_send.at[0],
            recv_sem=last_recv.at[0],
            device_id=device,
            device_id_type=MESH,
        )

    owners = smp_size // CHUNKS

    def close(c):
        for feeder in feeders_of(c, 0):
            pass_up(c, feeder).wait_recv()

        def block(yb, carry):
            whole = total_of(c, 0, yb, feeders_of(c, 0)).astype(BF16)
            for n in range(chunk_heads):
                final[c, n, yb] = whole[:, n * HEAD : (n + 1) * HEAD]
            return carry

        lax.fori_loop(0, Y_CHIPS, block, 0)
        first = c * owners
        turns = [
            (lax.rem(y + n // owners, Y_CHIPS), first + lax.rem(smp + n % owners, owners))
            for n in range(Y_CHIPS * owners)
        ]
        for py, ps in turns:

            @pl.when(py * smp_size + ps != mine)
            def _():
                last(c, (py * z_chips + z, ps), (ps - first) // 2, py, mine).start()

    def stores(c):
        narrow = pl.ds(c * cols, cols)
        wide = pl.ds(c * cols * group, cols * group)
        return [
            pltpu.make_async_copy(
                scratch.at[:, part_of], ref.at[0, :, part_of], store_sem.at[c, n]
            )
            for n, (scratch, ref, part_of) in enumerate(
                (
                    (dq_all, grad_queries_ref, wide),
                    (dk_own, grad_keys_ref, narrow),
                    (dv_own, grad_values_ref, narrow),
                )
            )
        ]

    begin(0)
    name(one_peer, pl.ds(0, others)).wait_recv()
    to_smem = pltpu.make_async_copy(named, named_s, smem_sem.at[0])
    to_smem.start()
    relay(0, 3)
    begin(1)
    relay(0, 6)
    relay(1, 3)
    to_smem.wait()
    leaves(0)
    middle = planes // 3
    send_picks(0, peers[:middle])
    relay(1, 6)
    send_picks(0, peers[middle:])
    leaves(1)
    send_picks(1, peers)
    for c in range(CHUNKS):
        keep_picks(c)
        held[c][TOP * planes] = jnp.zeros((rows, cols), BF16)
    lax.fori_loop(0, planes, locate, 0)
    where_copy = pltpu.make_async_copy(where_v, where_s, smem_sem.at[1])
    where_copy.start()
    for load in loads:
        load.wait()
    for c in range(CHUNKS):
        all_picks(c).wait_recv()
        grads(c)
        send_partials(c)
        for copy in stores(c):
            copy.start()
    where_copy.wait()
    all_partials(0).wait_recv()
    for role in UP_LEAVES:
        send_up(0, role)
        send_up(0, -role)
    send_up(0, 8 * eight(0))
    send_up(0, 6)
    send_up(0, -6)
    all_partials(1).wait_recv()
    for n, role in enumerate(UP_LEAVES):
        send_up(1, role)
        send_up(1, -role)
        if n == 1:
            send_up(1, 8 * eight(1))
            send_up(0, 3)
            send_up(0, -3)
    send_up(1, 6)
    send_up(1, -6)
    close(0)
    send_up(1, 3)
    send_up(1, -3)
    close(1)

    for c in range(CHUNKS):

        @pl.when(smp // owners == c)
        def _():
            gathered[mine] = final[c, (smp // 2) % chunk_heads, y]

    all_last = pltpu.make_async_remote_copy(
        src_ref=gathered.at[pl.ds(0, others)],
        dst_ref=gathered.at[pl.ds(0, others)],
        send_sem=last_send.at[0],
        recv_sem=last_recv.at[0],
        device_id=one_peer,
        device_id_type=MESH,
    )
    all_last.wait_recv()
    got_keys = gathered[:per_array].reshape(per_array * rows, HEAD).astype(F32)
    got_values = gathered[per_array:].reshape(per_array * rows, HEAD).astype(F32)
    low = lax.broadcasted_iota(jnp.int32, got_keys.shape, 1) < HEAD // 2
    even = jnp.where(low, got_keys, pltpu.roll(got_values, HEAD // 2, 1))
    odd = jnp.where(low, pltpu.roll(got_keys, HEAD // 2, 1), got_values)
    out_ref[...] = jnp.where(smp % 2 == 0, even, odd).T.astype(BF16)

    name(one_peer, pl.ds(0, others)).wait_send()
    for c in range(CHUNKS):
        for dy in range(1, Y_CHIPS):
            spread((y + dy) % Y_CHIPS, c, keys_ref).wait_send()
        for source, step in down_tree(c):
            pass_on(c, source, step).wait_send()
        for role, _ in up_tree(c):
            pass_up(c, role).wait_send()
        for copy in stores(c):
            copy.wait()
        all_picks(c).wait_send()
        all_partials(c).wait_send()
    all_last.wait_send()


def body(
    queries, out_grad, local_keys, trajectory_values, journal_keys, journal_values, picks, lengths
):
    smp_size = lax.axis_size("smp")
    z_chips = lax.axis_size("ctx") // Y_CHIPS
    planes = Y_CHIPS * smp_size
    block_rows, features = journal_keys.shape[1:]
    blocks = Y_CHIPS * z_chips
    rows = 2 * block_rows // planes
    cols = features // CHUNKS
    tq = queries.shape[1]
    width = queries.shape[2] // (features // HEAD) // HEAD * tq
    heads = cols // HEAD
    dma = pltpu.SemaphoreType.DMA
    vmem = pltpu.VMEM
    any_space = pl.BlockSpec(memory_space=pl.ANY)
    in_smem = pl.BlockSpec(memory_space=pltpu.SMEM)
    in_vmem = pl.BlockSpec(memory_space=pltpu.VMEM)
    grad_queries, grad_local_keys, grad_local_values, summed = pl.pallas_call(
        functools.partial(fused_kernel, z_chips, smp_size),
        out_shape=(
            jax.ShapeDtypeStruct(queries.shape, BF16),
            jax.ShapeDtypeStruct(local_keys.shape, BF16),
            jax.ShapeDtypeStruct(local_keys.shape, BF16),
            jax.ShapeDtypeStruct((HEAD, block_rows), BF16),
        ),
        in_specs=[in_smem, in_smem] + [any_space] * 6,
        out_specs=(any_space, any_space, any_space, in_vmem),
        scratch_shapes=[
            vmem((blocks, rows, cols), BF16),
            vmem((blocks, rows, cols), BF16),
            vmem((CHUNKS, planes, TOP, rows, cols), BF16),
            vmem((CHUNKS, planes, TOP, rows, cols), BF16),
            vmem((planes, 1, 128), jnp.int32),
            pltpu.SMEM((planes, 1, 128), jnp.int32),
            vmem((planes, 1, 128), jnp.int32),
            pltpu.SMEM((planes, 1, 128), jnp.int32),
            vmem(queries.shape[1:], BF16),
            vmem(queries.shape[1:], BF16),
            vmem(local_keys.shape[1:], BF16),
            vmem(local_keys.shape[1:], BF16),
            vmem(queries.shape[1:], BF16),
            vmem(local_keys.shape[1:], BF16),
            vmem(local_keys.shape[1:], BF16),
            vmem((TOP + 1, tq, width), F32),
            vmem((TOP + 1, tq, width), F32),
            vmem((CHUNKS, planes, TOP, rows, cols), BF16),
            vmem((TOP * planes + 1, rows, cols), BF16),
            vmem((TOP * planes + 1, rows, cols), BF16),
            vmem((CHUNKS, z_chips - 1, Y_CHIPS, rows, cols), BF16),
            vmem((CHUNKS, z_chips - 1, Y_CHIPS, rows, cols), BF16),
            vmem((CHUNKS, heads, Y_CHIPS, rows, HEAD), BF16),
            vmem((planes, rows, HEAD), BF16),
            dma((4,)),
            dma((CHUNKS, 3)),
            dma((CHUNKS, Y_CHIPS)),
            dma((CHUNKS, Y_CHIPS)),
            dma((CHUNKS,)),
            dma((1,)),
            dma((1,)),
            dma((2,)),
            dma((CHUNKS, z_chips - 1)),
            dma((CHUNKS, z_chips)),
            dma((CHUNKS,)),
            dma((CHUNKS,)),
            dma((CHUNKS,)),
            dma((CHUNKS,)),
            dma((CHUNKS, z_chips - 1)),
            dma((CHUNKS, z_chips - 1)),
            dma((1,)),
            dma((1,)),
        ],
        compiler_params=pltpu.CompilerParams(
            collective_id=0, has_side_effects=True, vmem_limit_bytes=56 << 20
        ),
        name="sparse_attention_grads",
    )(
        picks,
        lengths,
        queries,
        out_grad,
        local_keys,
        trajectory_values,
        journal_keys,
        journal_values,
    )
    return (
        grad_queries,
        grad_local_keys,
        grad_local_values,
        summed[: HEAD // 2].T[None],
        summed[HEAD // 2 :].T[None],
    )


def solution(mesh):
    in_specs = (
        P("smp", "ctx", None),
        P("smp", "ctx", None),
        P("smp", "ctx", None),
        P("smp", "ctx", None),
        P("ctx", None, None),
        P("ctx", None, None),
        P("smp", "ctx", None),
        P("smp"),
    )
    out_specs = (
        P("smp", "ctx", None),
        P("smp", "ctx", None),
        P("smp", "ctx", None),
        P("ctx", None, "smp"),
        P("ctx", None, "smp"),
    )
    return jax.shard_map(body, mesh=mesh, in_specs=in_specs, out_specs=out_specs, check_vma=False)
```

time: 142 us -> 112 us (0.79)
  Pallas kernels: 134 us -> 105 us
    pallas_call x1, Pallas kernels: 134 us -> 105 us  [body(): pl.pallas_call(functools.partial(fused_kernel, z_chips, smp_size), out_sh...]
    unnamed x9 -> x7, local copies, waits for them, and re-layouts: 5.52 us -> 4.1 us
where the time goes in v3:
time: 112 us
  Pallas kernels  105 us (94%)
  local copies, waits for them, and re-layouts  5.5 us (5%)
  between operations  1.29 us (1%)
    pallas_call x1, Pallas kernels, body(): pl.pallas_call(functools.partial(fused_kernel, z_chips, smp_size), out_sh...  105 us
    unnamed x7, local copies, waits for them, and re-layouts  4.1 us

profile of v3, /device:TPU:7, one launch (start us, length us, event | category | flops | bytes accessed | tf_op | source)
XLA Modules:
  0.0 112.0 jit_solution(15800902932107668236)
XLA Ops:
  1.3 105.2 %sparse_attention_grads.1 = (bf16[1,256,2048]{2,1,0:T(8,128)(2,1)}, bf16[1,256,512]{2,1,0:T(8,128)(2,1)}, bf16[1,256,512]{2,1,0:T(8,128)(2,1)}, bf16[128,256]{1,0:T(8,128)(2,1)}) custom-call(s32[1,1,3]{2,1,0:T(1,128)} %picks_ref.1, s32[1]{0:T(128)S(6)} %copy.16.length_ref, bf16[1,256,2048]{2,1,0:T(8,128)(2,1)} %queries_ref.1, ...), custom_call_target="tpu_custom_call" | custom-call | tf_op jit(solution)/shard_map/sparse_attention_grads/pallas_call | solution.py:614
  106.5 1.4 %slice_bitcast_fusion = (bf16[1,256,64]{1,2,0:T(8,128)(2,1)}, bf16[1,256,64]{1,2,0:T(8,128)(2,1)}) fusion(bf16[128,256]{1,0:T(8,128)(2,1)} %get-tuple-element.12), kind=kLoop, calls=%fused_computation | loop fusion | bytes 131072 | tf_op jit(solution)/shard_map/broadcast_in_dim | solution.py:687
  107.9 0.0 copy-start.1
  107.9 2.3 %copy.17 = bf16[1,256,2048]{2,1,0:T(8,128)(2,1)} copy(bf16[1,256,2048]{2,1,0:T(8,128)(2,1)} %get-tuple-element.20) | data formatting | bytes 2097152
  110.2 0.0 copy-done.1
  110.2 0.0 copy-start
  110.2 0.7 copy.18
  111.0 0.3 copy-done
  111.3 0.7 copy.19
Async XLA Ops:
  107.9 2.4 %copy-start.1 = (bf16[1,256,512]{2,1,0:T(8,128)(2,1)S(1)}, bf16[1,256,512]{2,1,0:T(8,128)(2,1)}, u32[]{:S(2)}) copy-start(bf16[1,256,512]{2,1,0:T(8,128)(2,1)} %get-tuple-element.21) | copy-start | bytes 786436
  110.2 1.0 copy-start

commit v4 on v3

--- a/solution.py
+++ b/solution.py
@@ -11,6 +11,7 @@
 HEAD = 128
 Y_CHIPS = 4
 SCALE = 1.0 / math.sqrt(HEAD)
+LOG2_E = math.log2(math.e)
 CHUNKS = 2
 TOP = 3
 MESH = pl.DeviceIdType.MESH
@@ -98,8 +99,8 @@
     fetched,
     named,
     named_s,
-    where_v,
-    where_s,
+    chosen,
+    sums,
     q_all,
     g_all,
     k_own,
@@ -279,12 +280,28 @@
                 arrived(c, distance * side)
         arrived(c, 8 * eight(c))
 
-    def locate(k, carry):
-        found = jnp.full((1, 128), TOP * planes, jnp.int32)
-        for i in range(TOP):
-            found = jnp.where(lane == named_s[k, 0, i], TOP * k + i, found)
-        where_v[k] = found
-        return carry
+    def choose():
+        lane_of = lax.broadcasted_iota(jnp.int32, (1, 128), 1)
+        slot, row = lane_of // rows, lane_of % rows
+        per_vector = 128 // rows
+        codes = []
+        for first in range(0, TOP * planes, per_vector):
+            code = jnp.zeros((1, 128), jnp.int32)
+            for j in range(per_vector):
+                pick = place_of((first + j) // TOP, (first + j) % TOP)
+                code = jnp.where(slot == j, pick * rows, code)
+            codes.append(code + row)
+        step = Y_CHIPS * rows
+
+        def one(n, carry):
+            start = pl.multiple_of(n * step, step)
+            number = lax.broadcasted_iota(jnp.int32, (step, 128), 0) + start
+            for m, code in enumerate(codes):
+                hit = jnp.where(number == code, 1.0, 0.0)
+                chosen[pl.ds(start, step), m * 128 : (m + 1) * 128] = hit.astype(BF16)
+            return carry
+
+        lax.fori_loop(0, z_chips, one, 0)
 
     def give(c, device, slot_send, slot_recv):
         return pltpu.make_async_remote_copy(
@@ -354,7 +371,7 @@
             total = jnp.zeros((1, width), F32)
             delta = jnp.zeros((1, width), F32)
             for i in range(TOP + 1):
-                w = jnp.exp((scores[i] - top) * SCALE)
+                w = jnp.exp2((scores[i] - top) * (SCALE * LOG2_E))
                 scores[i] = w
                 total = total + jnp.sum(w, axis=0, keepdims=True)
                 delta = delta + jnp.sum(w * grad_probs[i], axis=0, keepdims=True)
@@ -408,13 +425,24 @@
             device_id_type=MESH,
         )
 
-    def total_of(c, role, yb, feeders):
-        b = yb * z_chips + lax.rem(z + (z_chips - role) % z_chips, z_chips)
-        acc = held[c][where_s[0, 0, b]].astype(F32)
-        for k in range(1, planes):
-            acc = acc + held[c][where_s[k, 0, b]].astype(F32)
+    def add_up(c):
+        step = 4 * Y_CHIPS * rows
+        those = held[c][...].reshape(TOP * planes * rows, cols)
+
+        def one(n, carry):
+            part = pl.ds(pl.multiple_of(n * step, step), step)
+            sums[c, part] = jnp.dot(chosen[part], those, preferred_element_type=F32)
+            return carry
+
+        lax.fori_loop(0, z_chips // 4, one, 0)
+
+    def total_of(c, role, feeders):
+        step = Y_CHIPS * rows
+        dest = lax.rem(z + (z_chips - role) % z_chips, z_chips)
+        acc = sums[c, pl.ds(pl.multiple_of(dest * step, step), step)]
+        acc = acc.reshape(Y_CHIPS, rows, cols)
         for feeder in feeders:
-            acc = acc + arriving[c, slot_of(c, feeder), yb].astype(F32)
+            acc = acc + arriving[c, slot_of(c, feeder)].astype(F32)
         return acc
 
     def slot_of(c, role):
@@ -446,11 +474,7 @@
         for feeder in feeders:
             pass_up(c, feeder).wait_recv()
 
-        def block(yb, carry):
-            sending[c, slot, yb] = total_of(c, role, yb, feeders).astype(BF16)
-            return carry
-
-        lax.fori_loop(0, Y_CHIPS, block, 0)
+        sending[c, slot] = total_of(c, role, feeders).astype(BF16)
         pass_up(c, role).start()
 
     def last(c, device, head, py, slot_recv):
@@ -469,13 +493,9 @@
         for feeder in feeders_of(c, 0):
             pass_up(c, feeder).wait_recv()
 
-        def block(yb, carry):
-            whole = total_of(c, 0, yb, feeders_of(c, 0)).astype(BF16)
-            for n in range(chunk_heads):
-                final[c, n, yb] = whole[:, n * HEAD : (n + 1) * HEAD]
-            return carry
-
-        lax.fori_loop(0, Y_CHIPS, block, 0)
+        whole = total_of(c, 0, feeders_of(c, 0)).astype(BF16)
+        for n in range(chunk_heads):
+            final[c, n] = whole[:, :, n * HEAD : (n + 1) * HEAD]
         first = c * owners
         turns = [
             (lax.rem(y + n // owners, Y_CHIPS), first + lax.rem(smp + n % owners, owners))
@@ -521,10 +541,7 @@
     send_picks(1, peers)
     for c in range(CHUNKS):
         keep_picks(c)
-        held[c][TOP * planes] = jnp.zeros((rows, cols), BF16)
-    lax.fori_loop(0, planes, locate, 0)
-    where_copy = pltpu.make_async_copy(where_v, where_s, smem_sem.at[1])
-    where_copy.start()
+    choose()
     for load in loads:
         load.wait()
     for c in range(CHUNKS):
@@ -533,8 +550,8 @@
         send_partials(c)
         for copy in stores(c):
             copy.start()
-    where_copy.wait()
     all_partials(0).wait_recv()
+    add_up(0)
     for role in UP_LEAVES:
         send_up(0, role)
         send_up(0, -role)
@@ -542,6 +559,7 @@
     send_up(0, 6)
     send_up(0, -6)
     all_partials(1).wait_recv()
+    add_up(1)
     for n, role in enumerate(UP_LEAVES):
         send_up(1, role)
         send_up(1, -role)
@@ -628,8 +646,8 @@
             vmem((CHUNKS, planes, TOP, rows, cols), BF16),
             vmem((planes, 1, 128), jnp.int32),
             pltpu.SMEM((planes, 1, 128), jnp.int32),
-            vmem((planes, 1, 128), jnp.int32),
-            pltpu.SMEM((planes, 1, 128), jnp.int32),
+            vmem((blocks * rows, TOP * planes * rows), BF16),
+            vmem((CHUNKS, blocks * rows, cols), F32),
             vmem(queries.shape[1:], BF16),
             vmem(queries.shape[1:], BF16),
             vmem(local_keys.shape[1:], BF16),
@@ -640,8 +658,8 @@
             vmem((TOP + 1, tq, width), F32),
             vmem((TOP + 1, tq, width), F32),
             vmem((CHUNKS, planes, TOP, rows, cols), BF16),
-            vmem((TOP * planes + 1, rows, cols), BF16),
-            vmem((TOP * planes + 1, rows, cols), BF16),
+            vmem((TOP * planes, rows, cols), BF16),
+            vmem((TOP * planes, rows, cols), BF16),
             vmem((CHUNKS, z_chips - 1, Y_CHIPS, rows, cols), BF16),
             vmem((CHUNKS, z_chips - 1, Y_CHIPS, rows, cols), BF16),
             vmem((CHUNKS, heads, Y_CHIPS, rows, HEAD), BF16),

time: 112 us -> 115 us (1.027)
  Pallas kernels: 105 us -> 107 us
    pallas_call x1, Pallas kernels: 105 us -> 107 us  [body(): pl.pallas_call(functools.partial(fused_kernel, z_chips, smp_size), out_sh...]
where the time goes in v4:
time: 115 us; the launch traced here: 114 us
  Pallas kernels  107 us (93%)
  local copies, waits for them, and re-layouts  5.5 us (5%)
  between operations  1.29 us (1%)
    pallas_call x1, Pallas kernels, body(): pl.pallas_call(functools.partial(fused_kernel, z_chips, smp_size), out_sh...  107 us
    unnamed x7, local copies, waits for them, and re-layouts  4.1 us

profile of v4, /device:TPU:7, one launch (start us, length us, event | category | flops | bytes accessed | tf_op | source)
XLA Modules:
  0.0 114.2 jit_solution(15285207944552775980)
XLA Ops:
  1.3 107.5 %sparse_attention_grads.1 = (bf16[1,256,2048]{2,1,0:T(8,128)(2,1)}, bf16[1,256,512]{2,1,0:T(8,128)(2,1)}, bf16[1,256,512]{2,1,0:T(8,128)(2,1)}, bf16[128,256]{1,0:T(8,128)(2,1)}) custom-call(s32[1,1,3]{2,1,0:T(1,128)} %picks_ref.1, s32[1]{0:T(128)S(6)} %copy.16.length_ref, bf16[1,256,2048]{2,1,0:T(8,128)(2,1)} %queries_ref.1, ...), custom_call_target="tpu_custom_call" | custom-call | tf_op jit(solution)/shard_map/sparse_attention_grads/pallas_call | solution.py:632
  108.7 1.4 %slice_bitcast_fusion = (bf16[1,256,64]{1,2,0:T(8,128)(2,1)}, bf16[1,256,64]{1,2,0:T(8,128)(2,1)}) fusion(bf16[128,256]{1,0:T(8,128)(2,1)} %get-tuple-element.12), kind=kLoop, calls=%fused_computation | loop fusion | bytes 131072 | tf_op jit(solution)/shard_map/broadcast_in_dim | solution.py:705
  110.1 0.0 copy-start.1
  110.2 2.3 %copy.17 = bf16[1,256,2048]{2,1,0:T(8,128)(2,1)} copy(bf16[1,256,2048]{2,1,0:T(8,128)(2,1)} %get-tuple-element.20) | data formatting | bytes 2097152
  112.5 0.0 copy-done.1
  112.5 0.0 copy-start
  112.5 0.7 copy.18
  113.2 0.3 copy-done
  113.5 0.7 copy.19
Async XLA Ops:
  110.1 2.4 %copy-start.1 = (bf16[1,256,512]{2,1,0:T(8,128)(2,1)S(1)}, bf16[1,256,512]{2,1,0:T(8,128)(2,1)}, u32[]{:S(2)}) copy-start(bf16[1,256,512]{2,1,0:T(8,128)(2,1)} %get-tuple-element.21) | copy-start | bytes 786436
  112.5 1.0 copy-start

commit v5 on v4

--- a/solution.py
+++ b/solution.py
@@ -12,7 +12,7 @@
 Y_CHIPS = 4
 SCALE = 1.0 / math.sqrt(HEAD)
 LOG2_E = math.log2(math.e)
-CHUNKS = 2
+CHUNKS = 4
 TOP = 3
 MESH = pl.DeviceIdType.MESH
 BF16 = jnp.bfloat16
@@ -95,6 +95,8 @@
     out_ref,
     log_0,
     log_1,
+    log_2,
+    log_3,
     staged,
     fetched,
     named,
@@ -111,8 +113,7 @@
     scores,
     grad_probs,
     strips,
-    held_0,
-    held_1,
+    held,
     sending,
     arriving,
     final,
@@ -141,8 +142,7 @@
     mine = y * smp_size + smp
     peers = plane_of(y, z, smp, z_chips, smp_size)
     others = planes - 1
-    log = (log_0, log_1)
-    held = (held_0, held_1)
+    log = (log_0, log_1, log_2, log_3)
     rows, cols = log_0.shape[1:]
     per_array = planes // 2
     chunk_heads = cols // HEAD
@@ -402,7 +402,7 @@
     def back(c, device, slot_send, slot_recv):
         return pltpu.make_async_remote_copy(
             src_ref=strips.at[c, slot_send],
-            dst_ref=held[c].at[slot_recv],
+            dst_ref=held.at[c, slot_recv],
             send_sem=give_send.at[c],
             recv_sem=give_recv.at[c],
             device_id=device,
@@ -413,12 +413,12 @@
         for device, target in peers:
             back(c, device, target, pl.ds(TOP * mine, TOP)).start()
         for i in range(TOP):
-            held[c][TOP * mine + i] = strips[c, mine, i]
+            held[c, TOP * mine + i] = strips[c, mine, i]
 
     def all_partials(c):
         return pltpu.make_async_remote_copy(
-            src_ref=held[c].at[pl.ds(0, TOP * others)],
-            dst_ref=held[c].at[pl.ds(0, TOP * others)],
+            src_ref=held.at[c, pl.ds(0, TOP * others)],
+            dst_ref=held.at[c, pl.ds(0, TOP * others)],
             send_sem=give_send.at[c],
             recv_sem=give_recv.at[c],
             device_id=one_peer,
@@ -427,7 +427,7 @@
 
     def add_up(c):
         step = 4 * Y_CHIPS * rows
-        those = held[c][...].reshape(TOP * planes * rows, cols)
+        those = held[c].reshape(TOP * planes * rows, cols)
 
         def one(n, carry):
             part = pl.ds(pl.multiple_of(n * step, step), step)
@@ -508,8 +508,8 @@
                 last(c, (py * z_chips + z, ps), (ps - first) // 2, py, mine).start()
 
     def stores(c):
-        narrow = pl.ds(c * cols, cols)
-        wide = pl.ds(c * cols * group, cols * group)
+        narrow = pl.ds(pl.multiple_of(c * cols, cols), cols)
+        wide = pl.ds(pl.multiple_of(c * cols * group, cols), cols * group)
         return [
             pltpu.make_async_copy(
                 scratch.at[:, part_of], ref.at[0, :, part_of], store_sem.at[c, n]
@@ -527,52 +527,48 @@
     name(one_peer, pl.ds(0, others)).wait_recv()
     to_smem = pltpu.make_async_copy(named, named_s, smem_sem.at[0])
     to_smem.start()
-    relay(0, 3)
-    begin(1)
-    relay(0, 6)
-    relay(1, 3)
-    to_smem.wait()
-    leaves(0)
-    middle = planes // 3
-    send_picks(0, peers[:middle])
-    relay(1, 6)
-    send_picks(0, peers[middle:])
-    leaves(1)
-    send_picks(1, peers)
-    for c in range(CHUNKS):
-        keep_picks(c)
+    for stage in range(CHUNKS + 3):
+        if stage == 2:
+            to_smem.wait()
+        if 0 <= stage - 2 < CHUNKS:
+            relay(stage - 2, 6)
+        if 0 <= stage - 1 < CHUNKS:
+            relay(stage - 1, 3)
+        if 0 < stage < CHUNKS:
+            begin(stage)
+        if 0 <= stage - 3 < CHUNKS:
+            leaves(stage - 3)
+            send_picks(stage - 3, peers)
+            keep_picks(stage - 3)
     choose()
     for load in loads:
         load.wait()
-    for c in range(CHUNKS):
+
+    def heads(c, carry):
         all_picks(c).wait_recv()
         grads(c)
         send_partials(c)
         for copy in stores(c):
             copy.start()
-    all_partials(0).wait_recv()
-    add_up(0)
-    for role in UP_LEAVES:
-        send_up(0, role)
-        send_up(0, -role)
-    send_up(0, 8 * eight(0))
-    send_up(0, 6)
-    send_up(0, -6)
-    all_partials(1).wait_recv()
-    add_up(1)
-    for n, role in enumerate(UP_LEAVES):
-        send_up(1, role)
-        send_up(1, -role)
-        if n == 1:
-            send_up(1, 8 * eight(1))
-            send_up(0, 3)
-            send_up(0, -3)
-    send_up(1, 6)
-    send_up(1, -6)
-    close(0)
-    send_up(1, 3)
-    send_up(1, -3)
-    close(1)
+        return carry
+
+    lax.fori_loop(0, CHUNKS, heads, 0)
+    for stage in range(CHUNKS + 3):
+        if 0 <= stage < CHUNKS:
+            all_partials(stage).wait_recv()
+            add_up(stage)
+            for role in UP_LEAVES:
+                send_up(stage, role)
+                send_up(stage, -role)
+            send_up(stage, 8 * eight(stage))
+        if 0 <= stage - 1 < CHUNKS:
+            send_up(stage - 1, 6)
+            send_up(stage - 1, -6)
+        if 0 <= stage - 2 < CHUNKS:
+            send_up(stage - 2, 3)
+            send_up(stage - 2, -3)
+        if 0 <= stage - 3 < CHUNKS:
+            close(stage - 3)
 
     for c in range(CHUNKS):
 
@@ -609,6 +605,22 @@
         all_picks(c).wait_send()
         all_partials(c).wait_send()
     all_last.wait_send()
+
+
+def hand_over_kernel(grad_queries, grad_keys, grad_values, summed, *rest):
+    outs, sem = rest[:5], rest[5]
+    quarter = grad_queries.shape[1] // 4
+    parts = [
+        (grad_queries.at[:, n * quarter : (n + 1) * quarter], outs[0].at[:, n * quarter : (n + 1) * quarter])
+        for n in range(4)
+    ]
+    parts += [(grad_keys, outs[1]), (grad_values, outs[2])]
+    parts += [(summed.at[: HEAD // 2], outs[3]), (summed.at[HEAD // 2 :], outs[4])]
+    copies = [pltpu.make_async_copy(a, b, sem.at[n]) for n, (a, b) in enumerate(parts)]
+    for copy in copies:
+        copy.start()
+    for copy in copies:
+        copy.wait()
 
 
 def body(
@@ -642,6 +654,8 @@
         scratch_shapes=[
             vmem((blocks, rows, cols), BF16),
             vmem((blocks, rows, cols), BF16),
+            vmem((blocks, rows, cols), BF16),
+            vmem((blocks, rows, cols), BF16),
             vmem((CHUNKS, planes, TOP, rows, cols), BF16),
             vmem((CHUNKS, planes, TOP, rows, cols), BF16),
             vmem((planes, 1, 128), jnp.int32),
@@ -658,8 +672,7 @@
             vmem((TOP + 1, tq, width), F32),
             vmem((TOP + 1, tq, width), F32),
             vmem((CHUNKS, planes, TOP, rows, cols), BF16),
-            vmem((TOP * planes, rows, cols), BF16),
-            vmem((TOP * planes, rows, cols), BF16),
+            vmem((CHUNKS, TOP * planes, rows, cols), BF16),
             vmem((CHUNKS, z_chips - 1, Y_CHIPS, rows, cols), BF16),
             vmem((CHUNKS, z_chips - 1, Y_CHIPS, rows, cols), BF16),
             vmem((CHUNKS, heads, Y_CHIPS, rows, HEAD), BF16),
@@ -697,13 +710,23 @@
         journal_keys,
         journal_values,
     )
-    return (
-        grad_queries,
-        grad_local_keys,
-        grad_local_values,
-        summed[: HEAD // 2].T[None],
-        summed[HEAD // 2 :].T[None],
-    )
+    half_head = jax.ShapeDtypeStruct((HEAD // 2, block_rows), BF16)
+    results = pl.pallas_call(
+        hand_over_kernel,
+        out_shape=(
+            jax.ShapeDtypeStruct(queries.shape, BF16),
+            jax.ShapeDtypeStruct(local_keys.shape, BF16),
+            jax.ShapeDtypeStruct(local_keys.shape, BF16),
+            half_head,
+            half_head,
+        ),
+        in_specs=[any_space] * 4,
+        out_specs=(any_space,) * 5,
+        scratch_shapes=[dma((8,))],
+        compiler_params=pltpu.CompilerParams(vmem_limit_bytes=56 << 20),
+        name="hand_over",
+    )(grad_queries, grad_local_keys, grad_local_values, summed)
+    return results[:3] + (results[3].T[None], results[4].T[None])
 
 
 def solution(mesh):

time: 115 us -> 156 us (1.36)
  Pallas kernels: 107 us -> 154 us
  local copies, waits for them, and re-layouts: 5.5 us -> 0 us
    pallas_call x0 -> x1, Pallas kernels: none -> 50.8 us  [body(): pl.pallas_call(hand_over_kernel, out_shape=(jax.ShapeDtypeStruct(queries....]
    unnamed x7 -> x0, local copies, waits for them, and re-layouts: 4.1 us -> none
    pallas_call x1, Pallas kernels: 107 us -> 104 us  [body(): pl.pallas_call(functools.partial(fused_kernel, z_chips, smp_size), out_sh...]
where the time goes in v5:
time: 156 us
  Pallas kernels  154 us (99%)
    pallas_call x1, Pallas kernels, body(): pl.pallas_call(functools.partial(fused_kernel, z_chips, smp_size), out_sh...  104 us
    pallas_call x1, Pallas kernels, body(): pl.pallas_call(hand_over_kernel, out_shape=(jax.ShapeDtypeStruct(queries....  50.8 us

profile of v5, /device:TPU:7, one launch (start us, length us, event | category | flops | bytes accessed | tf_op | source)
XLA Modules:
  0.0 155.8 jit_solution(15817524296306036917)
XLA Ops:
  1.3 103.7 %sparse_attention_grads.1 = (bf16[1,256,2048]{2,1,0:T(8,128)(2,1)}, bf16[1,256,512]{2,1,0:T(8,128)(2,1)}, bf16[1,256,512]{2,1,0:T(8,128)(2,1)}, bf16[128,256]{1,0:T(8,128)(2,1)}) custom-call(s32[1,1,3]{2,1,0:T(1,128)} %picks_ref.1, s32[1]{0:T(128)S(6)} %copy.13.length_ref, bf16[1,256,2048]{2,1,0:T(8,128)(2,1)} %queries_ref.1, ...), custom_call_target="tpu_custom_call" | custom-call | tf_op jit(solution)/shard_map/sparse_attention_grads/pallas_call | solution.py:644
  105.0 50.8 %hand_over.1 = (bf16[1,256,2048]{2,1,0:T(8,128)(2,1)}, bf16[1,256,512]{2,1,0:T(8,128)(2,1)}, bf16[1,256,512]{2,1,0:T(8,128)(2,1)}, bf16[64,256]{1,0:T(8,128)(2,1)}, bf16[64,256]{1,0:T(8,128)(2,1)}) custom-call(bf16[1,256,2048]{2,1,0:T(8,128)(2,1)} %get-tuple-element.14.grad_queries, bf16[1,256,512]{2,1,0:T(8,128)(2,1)} %get-tuple-element.15.grad_keys, ...), custom_call_target="tpu_custom_call" | custom-call | tf_op jit(solution)/shard_map/hand_over/pallas_call | solution.py:714

commit v6 on v5

--- a/solution.py
+++ b/solution.py
@@ -41,7 +41,7 @@
                         along_y[dy] * smp_size + along_smp[ds],
                     )
                 )
-    return peers
+    return [peers[(12 * n) % len(peers)] for n in range(len(peers))]
 
 
 def enter(y, z, smp, z_chips, peers):
@@ -607,20 +607,34 @@
     all_last.wait_send()
 
 
-def hand_over_kernel(grad_queries, grad_keys, grad_values, summed, *rest):
-    outs, sem = rest[:5], rest[5]
-    quarter = grad_queries.shape[1] // 4
-    parts = [
-        (grad_queries.at[:, n * quarter : (n + 1) * quarter], outs[0].at[:, n * quarter : (n + 1) * quarter])
-        for n in range(4)
+def hand_over_kernel(
+    grad_queries, grad_keys, grad_values, summed, out_q, out_k, out_v, out_gk, out_gv, q, k, v, both,
+    load_sem, store_sem
+):
+    quarter = q.shape[1] // 4
+    steps = []
+    for n in range(4):
+        rows = pl.ds(n * quarter, quarter)
+        steps.append((grad_queries.at[:, rows], q.at[:, rows], out_q.at[:, rows]))
+    steps.append((grad_keys, k, out_k))
+    steps.append((grad_values, v, out_v))
+    steps.append((summed.at[: HEAD // 2], both.at[: HEAD // 2], out_gk))
+    steps.append((summed.at[HEAD // 2 :], both.at[HEAD // 2 :], out_gv))
+    loads = [
+        pltpu.make_async_copy(source, held, load_sem.at[n])
+        for n, (source, held, _) in enumerate(steps)
     ]
-    parts += [(grad_keys, outs[1]), (grad_values, outs[2])]
-    parts += [(summed.at[: HEAD // 2], outs[3]), (summed.at[HEAD // 2 :], outs[4])]
-    copies = [pltpu.make_async_copy(a, b, sem.at[n]) for n, (a, b) in enumerate(parts)]
-    for copy in copies:
-        copy.start()
-    for copy in copies:
-        copy.wait()
+    stores = [
+        pltpu.make_async_copy(held, target, store_sem.at[n])
+        for n, (_, held, target) in enumerate(steps)
+    ]
+    for load in loads:
+        load.start()
+    for load, store in zip(loads, stores):
+        load.wait()
+        store.start()
+    for store in stores:
+        store.wait()
 
 
 def body(
@@ -722,7 +736,14 @@
         ),
         in_specs=[any_space] * 4,
         out_specs=(any_space,) * 5,
-        scratch_shapes=[dma((8,))],
+        scratch_shapes=[
+            vmem(queries.shape, BF16),
+            vmem(local_keys.shape, BF16),
+            vmem(local_keys.shape, BF16),
+            vmem((HEAD, block_rows), BF16),
+            dma((8,)),
+            dma((8,)),
+        ],
         compiler_params=pltpu.CompilerParams(vmem_limit_bytes=56 << 20),
         name="hand_over",
     )(grad_queries, grad_local_keys, grad_local_values, summed)

time: 156 us -> 108 us (0.69)
  Pallas kernels: 154 us -> 107 us
    pallas_call x1, Pallas kernels: 50.8 us -> 2.23 us  [body(): pl.pallas_call(hand_over_kernel, out_shape=(jax.ShapeDtypeStruct(queries....]
where the time goes in v6:
time: 108 us
  Pallas kernels  107 us (99%)
  between operations  1.29 us (1%)
    pallas_call x1, Pallas kernels, body(): pl.pallas_call(functools.partial(fused_kernel, z_chips, smp_size), out_sh...  104 us
    pallas_call x1, Pallas kernels, body(): pl.pallas_call(hand_over_kernel, out_shape=(jax.ShapeDtypeStruct(queries....  2.23 us

profile of v6, /device:TPU:7, one launch (start us, length us, event | category | flops | bytes accessed | tf_op | source)
XLA Modules:
  0.0 108.0 jit_solution(8178005922241476826)
XLA Ops:
  1.3 104.5 %sparse_attention_grads.1 = (bf16[1,256,2048]{2,1,0:T(8,128)(2,1)}, bf16[1,256,512]{2,1,0:T(8,128)(2,1)}, bf16[1,256,512]{2,1,0:T(8,128)(2,1)}, bf16[128,256]{1,0:T(8,128)(2,1)}) custom-call(s32[1,1,3]{2,1,0:T(1,128)} %picks_ref.1, s32[1]{0:T(128)S(6)} %copy.13.length_ref, bf16[1,256,2048]{2,1,0:T(8,128)(2,1)} %queries_ref.1, ...), custom_call_target="tpu_custom_call" | custom-call | tf_op jit(solution)/shard_map/sparse_attention_grads/pallas_call | solution.py:658
  105.8 2.2 %hand_over.1 = (bf16[1,256,2048]{2,1,0:T(8,128)(2,1)}, bf16[1,256,512]{2,1,0:T(8,128)(2,1)}, bf16[1,256,512]{2,1,0:T(8,128)(2,1)}, bf16[64,256]{1,0:T(8,128)(2,1)}, bf16[64,256]{1,0:T(8,128)(2,1)}) custom-call(bf16[1,256,2048]{2,1,0:T(8,128)(2,1)} %get-tuple-element.14.grad_queries, bf16[1,256,512]{2,1,0:T(8,128)(2,1)} %get-tuple-element.15.grad_keys, ...), custom_call_target="tpu_custom_call" | custom-call | tf_op jit(solution)/shard_map/hand_over/pallas_call | solution.py:728

commit v7 on v6

--- a/solution.py
+++ b/solution.py
@@ -527,22 +527,33 @@
     name(one_peer, pl.ds(0, others)).wait_recv()
     to_smem = pltpu.make_async_copy(named, named_s, smem_sem.at[0])
     to_smem.start()
-    for stage in range(CHUNKS + 3):
+    def serve_picks(c):
+        leaves(c)
+        send_picks(c, peers)
+        keep_picks(c)
+
+    for stage in range(CHUNKS + 2):
         if stage == 2:
             to_smem.wait()
+            choose()
         if 0 <= stage - 2 < CHUNKS:
             relay(stage - 2, 6)
         if 0 <= stage - 1 < CHUNKS:
             relay(stage - 1, 3)
         if 0 < stage < CHUNKS:
             begin(stage)
-        if 0 <= stage - 3 < CHUNKS:
-            leaves(stage - 3)
-            send_picks(stage - 3, peers)
-            keep_picks(stage - 3)
-    choose()
+        if 0 <= stage - 3 < CHUNKS - 1:
+            serve_picks(stage - 3)
     for load in loads:
         load.wait()
+
+    def climb(c):
+        all_partials(c).wait_recv()
+        add_up(c)
+        for role in UP_LEAVES:
+            send_up(c, role)
+            send_up(c, -role)
+        send_up(c, 8 * eight(c))
 
     def heads(c, carry):
         all_picks(c).wait_recv()
@@ -550,17 +561,21 @@
         send_partials(c)
         for copy in stores(c):
             copy.start()
+
+        @pl.when(c == 0)
+        def _():
+            serve_picks(CHUNKS - 1)
+
+        @pl.when(c == CHUNKS - 2)
+        def _():
+            climb(0)
+
         return carry
 
     lax.fori_loop(0, CHUNKS, heads, 0)
-    for stage in range(CHUNKS + 3):
-        if 0 <= stage < CHUNKS:
-            all_partials(stage).wait_recv()
-            add_up(stage)
-            for role in UP_LEAVES:
-                send_up(stage, role)
-                send_up(stage, -role)
-            send_up(stage, 8 * eight(stage))
+    for stage in range(1, CHUNKS + 3):
+        if stage < CHUNKS:
+            climb(stage)
         if 0 <= stage - 1 < CHUNKS:
             send_up(stage - 1, 6)
             send_up(stage - 1, -6)

time: 108 us -> 104 us (0.963)
  Pallas kernels: 107 us -> 102 us
    pallas_call x1, Pallas kernels: 104 us -> 100 us  [body(): pl.pallas_call(functools.partial(fused_kernel, z_chips, smp_size), out_sh...]
where the time goes in v7:
time: 104 us
  Pallas kernels  102 us (98%)
  between operations  1.29 us (1%)
    pallas_call x1, Pallas kernels, body(): pl.pallas_call(functools.partial(fused_kernel, z_chips, smp_size), out_sh...  100 us
    pallas_call x1, Pallas kernels, body(): pl.pallas_call(hand_over_kernel, out_shape=(jax.ShapeDtypeStruct(queries....  2.23 us

profile of v7, /device:TPU:7, one launch (start us, length us, event | category | flops | bytes accessed | tf_op | source)
XLA Modules:
  0.0 103.6 jit_solution(17155450117051961494)
XLA Ops:
  1.3 100.1 %sparse_attention_grads.1 = (bf16[1,256,2048]{2,1,0:T(8,128)(2,1)}, bf16[1,256,512]{2,1,0:T(8,128)(2,1)}, bf16[1,256,512]{2,1,0:T(8,128)(2,1)}, bf16[128,256]{1,0:T(8,128)(2,1)}) custom-call(s32[1,1,3]{2,1,0:T(1,128)} %picks_ref.1, s32[1]{0:T(128)S(6)} %copy.13.length_ref, bf16[1,256,2048]{2,1,0:T(8,128)(2,1)} %queries_ref.1, ...), custom_call_target="tpu_custom_call" | custom-call | tf_op jit(solution)/shard_map/sparse_attention_grads/pallas_call | solution.py:673
  101.4 2.2 %hand_over.1 = (bf16[1,256,2048]{2,1,0:T(8,128)(2,1)}, bf16[1,256,512]{2,1,0:T(8,128)(2,1)}, bf16[1,256,512]{2,1,0:T(8,128)(2,1)}, bf16[64,256]{1,0:T(8,128)(2,1)}, bf16[64,256]{1,0:T(8,128)(2,1)}) custom-call(bf16[1,256,2048]{2,1,0:T(8,128)(2,1)} %get-tuple-element.14.grad_queries, bf16[1,256,512]{2,1,0:T(8,128)(2,1)} %get-tuple-element.15.grad_keys, ...), custom_call_target="tpu_custom_call" | custom-call | tf_op jit(solution)/shard_map/hand_over/pallas_call | solution.py:743

commit v8 on v7

--- a/solution.py
+++ b/solution.py
@@ -573,17 +573,19 @@
         return carry
 
     lax.fori_loop(0, CHUNKS, heads, 0)
-    for stage in range(1, CHUNKS + 3):
-        if stage < CHUNKS:
+    ahead = [1] + [0] * (CHUNKS - 1)
+    for stage in range(CHUNKS + 3):
+        if 0 < stage < CHUNKS:
             climb(stage)
-        if 0 <= stage - 1 < CHUNKS:
-            send_up(stage - 1, 6)
-            send_up(stage - 1, -6)
-        if 0 <= stage - 2 < CHUNKS:
-            send_up(stage - 2, 3)
-            send_up(stage - 2, -3)
-        if 0 <= stage - 3 < CHUNKS:
-            close(stage - 3)
+        for c in range(CHUNKS):
+            if stage == c + 1 - ahead[c]:
+                send_up(c, 6)
+                send_up(c, -6)
+            if stage == c + 2 - ahead[c]:
+                send_up(c, 3)
+                send_up(c, -3)
+            if stage == c + 3 - ahead[c]:
+                close(c)
 
     for c in range(CHUNKS):
 

time: 104 us -> 108 us (1.038)
  Pallas kernels: 102 us -> 106 us
    pallas_call x1, Pallas kernels: 100 us -> 104 us  [body(): pl.pallas_call(functools.partial(fused_kernel, z_chips, smp_size), out_sh...]
where the time goes in v8:
time: 108 us; the launch traced here: 107 us
  Pallas kernels  106 us (98%)
  between operations  1.29 us (1%)
    pallas_call x1, Pallas kernels, body(): pl.pallas_call(functools.partial(fused_kernel, z_chips, smp_size), out_sh...  104 us
    pallas_call x1, Pallas kernels, body(): pl.pallas_call(hand_over_kernel, out_shape=(jax.ShapeDtypeStruct(queries....  2.23 us

profile of v8, /device:TPU:7, one launch (start us, length us, event | category | flops | bytes accessed | tf_op | source)
XLA Modules:
  0.0 107.1 jit_solution(15380827333495459526)
XLA Ops:
  1.3 103.6 %sparse_attention_grads.1 = (bf16[1,256,2048]{2,1,0:T(8,128)(2,1)}, bf16[1,256,512]{2,1,0:T(8,128)(2,1)}, bf16[1,256,512]{2,1,0:T(8,128)(2,1)}, bf16[128,256]{1,0:T(8,128)(2,1)}) custom-call(s32[1,1,3]{2,1,0:T(1,128)} %picks_ref.1, s32[1]{0:T(128)S(6)} %copy.13.length_ref, bf16[1,256,2048]{2,1,0:T(8,128)(2,1)} %queries_ref.1, ...), custom_call_target="tpu_custom_call" | custom-call | tf_op jit(solution)/shard_map/sparse_attention_grads/pallas_call | solution.py:675
  104.9 2.2 %hand_over.1 = (bf16[1,256,2048]{2,1,0:T(8,128)(2,1)}, bf16[1,256,512]{2,1,0:T(8,128)(2,1)}, bf16[1,256,512]{2,1,0:T(8,128)(2,1)}, bf16[64,256]{1,0:T(8,128)(2,1)}, bf16[64,256]{1,0:T(8,128)(2,1)}) custom-call(bf16[1,256,2048]{2,1,0:T(8,128)(2,1)} %get-tuple-element.14.grad_queries, bf16[1,256,512]{2,1,0:T(8,128)(2,1)} %get-tuple-element.15.grad_keys, ...), custom_call_target="tpu_custom_call" | custom-call | tf_op jit(solution)/shard_map/hand_over/pallas_call | solution.py:745
